TPU v7x, 512 devices: a whole 4x4x16 slice. The times are simulated.
512 devices in a mesh: tmpl: 128 (over x, y, z_lo), det: 4 (over z_hi, core).
Axes of the slice: x: 4, y: 4, z: 16 (z_hi: 2, z_lo: 8; z = z_hi * 8 + z_lo), core: 2. Of those that a mesh axis runs over, the one named last changes fastest.
Arguments:
- templates: bfloat16 [2, 4, 1024, 1024], P(None, 'det', 'tmpl'), may hold values from -6 to 6
- strain: bfloat16 [2, 3, 1024, 1024], P(None, None, 'tmpl', 'det'), may hold values from -6 to 6
- inverse_psd: float32 [3, 1024, 1024], P(None, 'tmpl'), may hold values from 0.5 to 18.5
- antenna: float32 [3, 64], replicated, may hold values from -1 to 1
- delays: int32 [3, 64], replicated, may hold values from -8 to 8
Outputs:
- sky_max: float32 [4, 1024, 1024], P('det', 'tmpl')
- peak: float32 [4, 64], P('det')
All inputs are finite; a program needn't handle non-finite values.
Results may differ from a plain program's by a relative error of at most 0.0038.
Values may be sent and summed in bfloat16 or wider, within the bound.
A program may use at most 64 MiB of HBM per device.

v0:
```python
import math

import jax
import jax.numpy as jnp
from jax import lax
from jax.sharding import PartitionSpec as P

NU = 1024
DMAX = 8


def with_halo(cells, sides, width):
    for axis, dim in sides:
        count = lax.axis_size(axis)
        head = lax.slice_in_dim(cells, 0, width, axis=dim)
        tail = lax.slice_in_dim(cells, cells.shape[dim] - width, cells.shape[dim], axis=dim)
        cells = jnp.concatenate(
            [
                lax.ppermute(tail, axis, [(i, (i + 1) % count) for i in range(count)]),
                cells,
                lax.ppermute(head, axis, [((i + 1) % count, i) for i in range(count)]),
            ],
            axis=dim,
        )
    return cells


def dft_table(length):
    idx = jnp.arange(length, dtype=jnp.int32)
    phase_ids = idx[:, None] * idx[None, :] % length
    phases = phase_ids.astype(jnp.float32) * (2.0 * math.pi / length)
    return (jnp.cos(phases).astype(jnp.bfloat16), jnp.sin(phases).astype(jnp.bfloat16))


def second_section(received, cos_two, sin_two):
    form = "kdup,uq->kdpq"
    out_real = jnp.einsum(
        form, received[0], cos_two, preferred_element_type=jnp.float32
    ) - jnp.einsum(form, received[1], sin_two, preferred_element_type=jnp.float32)
    out_imag = jnp.einsum(
        form, received[0], sin_two, preferred_element_type=jnp.float32
    ) + jnp.einsum(form, received[1], cos_two, preferred_element_type=jnp.float32)
    return jnp.stack([out_real, out_imag])


def shards(templates, strain, inverse_psd, antenna, delays):
    full_strain = lax.all_gather(strain, "det", axis=3, tiled=True)
    count_tmpl = templates.shape[1]
    local_rows = templates.shape[2]
    inner_len = templates.shape[3]
    detectors = full_strain.shape[1]
    sky_count = antenna.shape[1]
    full_length = NU * inner_len
    tmpl_real = templates[0][:, None].astype(jnp.float32)
    tmpl_imag = templates[1][:, None].astype(jnp.float32)
    data_real = full_strain[0][None].astype(jnp.float32)
    data_imag = full_strain[1][None].astype(jnp.float32)
    psd_weight = inverse_psd[None]
    own_power = jnp.sum((tmpl_real * tmpl_real + tmpl_imag * tmpl_imag) * psd_weight, axis=(2, 3))
    sigma_sq = lax.psum(own_power, "tmpl")
    prod_real = ((tmpl_real * data_real + tmpl_imag * data_imag) * psd_weight).astype(jnp.bfloat16)
    prod_imag = ((tmpl_real * data_imag - tmpl_imag * data_real) * psd_weight).astype(jnp.bfloat16)
    cos_one, sin_one = dft_table(inner_len)
    cos_two, sin_two = dft_table(NU)
    flat_real = prod_real.reshape(-1, inner_len)
    flat_imag = prod_imag.reshape(-1, inner_len)
    section_real = jnp.dot(flat_real, cos_one, preferred_element_type=jnp.float32) - jnp.dot(
        flat_imag, sin_one, preferred_element_type=jnp.float32
    )
    section_imag = jnp.dot(flat_real, sin_one, preferred_element_type=jnp.float32) + jnp.dot(
        flat_imag, cos_one, preferred_element_type=jnp.float32
    )
    shape_four = (count_tmpl, detectors, local_rows, inner_len)
    section_real = section_real.reshape(shape_four)
    section_imag = section_imag.reshape(shape_four)
    row_ids = lax.axis_index("tmpl") * local_rows + jnp.arange(local_rows, dtype=jnp.int32)
    phase_ids = row_ids[:, None] * jnp.arange(inner_len, dtype=jnp.int32)[None, :] % full_length
    phases = phase_ids.astype(jnp.float32) * (2.0 * math.pi / full_length)
    twist_cos = jnp.cos(phases)
    twist_sin = jnp.sin(phases)
    twisted = jnp.stack(
        [
            section_real * twist_cos - section_imag * twist_sin,
            section_real * twist_sin + section_imag * twist_cos,
        ]
    ).astype(jnp.bfloat16)
    outputs = second_section(
        lax.all_to_all(twisted, "tmpl", split_axis=4, concat_axis=3, tiled=True), cos_two, sin_two
    )
    inverse_norm = 1.0 / jnp.sqrt(sigma_sq)
    filtered = outputs * inverse_norm[None, :, :, None, None]
    extended = with_halo(filtered, (("tmpl", 3),), DMAX)
    position = lax.axis_index("tmpl")
    final_index = lax.axis_size("tmpl") - 1
    total_rows = extended.shape[3]
    lower_rim = extended[:, :, :, :DMAX]
    middle_rows = extended[:, :, :, DMAX : total_rows - DMAX]
    upper_rim = extended[:, :, :, total_rows - DMAX :]
    lower_rim = jnp.where(position == 0, jnp.roll(lower_rim, 1, axis=4), lower_rim)
    upper_rim = jnp.where(position == final_index, jnp.roll(upper_rim, -1, axis=4), upper_rim)
    extended = jnp.concatenate([lower_rim, middle_rows, upper_rim], axis=3)
    rows_here = total_rows - 2 * DMAX

    def visit(best_power, sky_index):
        sum_real = jnp.zeros((count_tmpl, rows_here, NU), jnp.float32)
        sum_imag = jnp.zeros((count_tmpl, rows_here, NU), jnp.float32)
        for detector in range(detectors):
            offset_rows = DMAX + delays[detector, sky_index]
            shifted = lax.dynamic_slice_in_dim(
                extended[:, :, detector], offset_rows, rows_here, axis=2
            )
            antenna_gain = antenna[detector, sky_index]
            sum_real = sum_real + antenna_gain * shifted[0]
            sum_imag = sum_imag + antenna_gain * shifted[1]
        snr_power = sum_real * sum_real + sum_imag * sum_imag
        return (jnp.maximum(best_power, snr_power), jnp.max(snr_power, axis=(1, 2)))

    best_power, sky_peaks = lax.scan(
        visit,
        jnp.zeros((count_tmpl, rows_here, NU), jnp.float32),
        jnp.arange(sky_count, dtype=jnp.int32),
    )
    peak = lax.pmax(jnp.transpose(sky_peaks), "tmpl")
    return (best_power, peak)


def solution(mesh):
    return jax.shard_map(
        shards,
        mesh=mesh,
        in_specs=(
            P(None, "det", "tmpl", None),
            P(None, None, "tmpl", "det"),
            P(None, "tmpl", None),
            P(),
            P(),
        ),
        out_specs=(P("det", "tmpl", None), P("det", None)),
        check_vma=False,
    )
```

profile of v0, /device:TPU:32, one launch (start us, length us, event | category | flops | bytes accessed | tf_op | source)
XLA Modules:
  0.0 1952.3 jit_solution(4365366661310408854)
XLA Ops:
  1.4 16.5 all_gather.3
  18.8 15.7 fusion.22
  34.5 15.7 fusion.21
  50.2 16.6 fusion.26
  67.1 17.1 fusion.47
  88.6 16.8 all-to-all-start
  105.6 517.4 %psum.7 = f32[1,3]{1,0:T(1,128)S(1)} all-reduce(f32[1,3]{1,0:T(1,128)S(1)} %bitcast.115), channel_id=1, replica_groups=mesh['tmpl'=128,'det'=4] {'tmpl'}, use_global_device_ids=true, to_apply=%region_1.0 | all-reduce | flops 3 | bytes 24 | tf_op jit(solution)/shard_map/psum | solution.py:60
  624.2 4.2 copy.23
  631.2 15.8 fusion.15
  649.7 16.0 fusion.13
  665.7 15.7 fusion.32
  681.4 15.9 fusion.38
  697.5 14.3 collective-permute-start.1
  715.1 4.3 collective-permute-done
  719.7 704.9 %while.16 = (s32[]{:T(128)}, f32[1,8,1024]{2,1,0:T(8,128)S(1)}, f32[64,1]{0,1:T(1,128)S(1)}, s32[64]{0:T(128)S(1)}, f32[3,64]{1,0:T(4,128)S(1)}, /*index=5*/f32[...) while((s32[]{:T(128)}, f32[1,8,1024]{2,1,0:T(8,128)S(1)}, ...), condition=%wide.region_4.5_spmd.clone, body=%wide.region_2.4_spmd.clone.sunk | while | flops 131090 | bytes 1507759 | solution.py:118
  727.4 2.6 fusion.108
  738.4 2.6 fusion.108
  760.4 2.6 fusion.108
  782.4 2.6 fusion.108
  804.5 2.6 fusion.108
  826.5 2.6 fusion.108
  837.5 2.6 fusion.108
  848.5 2.6 fusion.108
  859.5 2.6 fusion.108
  870.5 2.6 fusion.108
  881.6 2.6 fusion.108
  903.6 2.6 fusion.108
  925.6 2.6 fusion.108
  947.6 2.6 fusion.108
  969.7 2.6 fusion.108
  991.7 2.6 fusion.108
  1424.6 527.5 %pmax.7 = f32[1,64]{1,0:T(1,128)} all-reduce(f32[1,64]{1,0:T(1,128)S(1)} %bitcast.116), channel_id=1, replica_groups=mesh['tmpl'=128,'det'=4] {'tmpl'}, use_global_device_ids=true, to_apply=%region_5.6 | all-reduce | flops 64 | bytes 512 | tf_op jit(solution)/shard_map/pmax | solution.py:123
  (471 shorter events, 312.4 us)
Async XLA Ops:
  84.2 21.2 %copy-start.2 = (bf16[2,1,8,1024]{3,2,1,0:T(8,128)(2,1)S(1)}, bf16[2,1,8,1024]{3,2,1,0:T(8,128)(2,1)}, u32[]{:S(2)}) copy-start(bf16[2,1,8,1024]{3,2,1,0:T(8,128)(2,1)} %param.7) | copy-start | bytes 98308
  84.2 21.2 %copy-start.1 = (f32[3,8,1024]{2,1,0:T(8,128)S(1)}, f32[3,8,1024]{2,1,0:T(8,128)}, u32[]{:S(2)}) copy-start(f32[3,8,1024]{2,1,0:T(8,128)} %param.9) | copy-start | bytes 294916
  88.6 534.4 %all-to-all-start = ((bf16[128,2,192]{2,1,0:T(2,128)(2,1)}), bf16[128,2,192]{2,1,0:T(2,128)(2,1)S(1)}, u32[]{:S(2)}, u32[]{:S(2)}) async-start(bf16[128,2,192]{2,1,0:T(2,128)(2,1)} %reshape.437), calls=%async_computation | async-start | bytes 262144 | tf_op jit(solution)/shard_map/all_to_all | solution.py:88
  697.3 22.3 %copy-start.3 = (f32[3,64]{1,0:T(4,128)S(1)}, f32[3,64]{1,0:T(4,128)}, u32[]{:S(2)}) copy-start(f32[3,64]{1,0:T(4,128)} %param.10) | copy-start | bytes 2308
  697.4 22.3 %copy-start.4 = (s32[3,64]{1,0:T(4,128)S(1)}, s32[3,64]{1,0:T(4,128)}, u32[]{:S(2)}) copy-start(s32[3,64]{1,0:T(4,128)} %param.11) | copy-start | bytes 2308
  697.5 17.5 collective-permute-start.1
  711.8 7.6 collective-permute-start
  1424.6 527.5 %copy-start = (f32[1,8,1024]{2,1,0:T(8,128)}, f32[1,8,1024]{2,1,0:T(8,128)S(1)}, u32[]{:S(2)}) copy-start(f32[1,8,1024]{2,1,0:T(8,128)S(1)} %get-tuple-element.111) | copy-start | bytes 98308
where the time goes:
time: 1970 us; the launch traced here: 1950 us
  blocking collectives  1060 us (54%)
  loops' own time  368 us (19%)
  local copies, waits for them, and re-layouts  187 us (9%)
  other arithmetic  168 us (9%)
  matrix products  129 us (7%)
  starting transfers between devices  33.1 us (2%)
    pmax x1, blocking collectives, shards(): peak = lax.pmax(jnp.transpose(sky_peaks), 'tmpl')  527 us
    psum x1, blocking collectives, shards(): sigma_sq = lax.psum(own_power, 'tmpl')  517 us
    another operation x1, loops' own time, shards(): lax.scan(visit, jnp.zeros((count_tmpl, rows_here, NU), jnp.float32), jnp....  368 us
    reduce_max x64, other arithmetic, visit(): return (jnp.maximum(best_power, snr_power), jnp.max(snr_power, axis=(1, 2)))  165 us
    dynamic_update_slice x64, local copies, waits for them, and re-layouts, shards(): lax.scan(visit, jnp.zeros((count_tmpl, rows_here, NU), jnp.float32), jnp....  46.8 us
    dynamic_slice x64, local copies, waits for them, and re-layouts, visit(): antenna_gain = antenna[detector, sky_index]  42.3 us
    dynamic_slice x64, local copies, waits for them, and re-layouts, visit(): offset_rows = DMAX + delays[detector, sky_index]  41.9 us
  transfers between devices with their start and end apart: 3, of which 2 were waited for; matrix products, arithmetic and copies ran while one was open for 0% of the time, Pallas kernels for 0%

commit v1 on v0

v1 whole, which is shorter than its diff:
```python
import math

import jax
import jax.numpy as jnp
import ml_dtypes
import numpy as np
from jax import lax
from jax.experimental import pallas as pl
from jax.experimental.pallas import tpu as pltpu
from jax.sharding import PartitionSpec as P

F32 = jnp.float32
BF16 = jnp.bfloat16
MESH = pl.DeviceIdType.MESH

LEN = 1024
FULL = LEN * LEN
DET = 3
SKY = 64
HALO = 8
CELLS = 16
ZS = 8
GROUPS = 4
ROWS = 8
WIDE = 64 + 2 * HALO
COLS = CELLS * WIDE
CHUNK = 256
NCHUNK = COLS // CHUNK
SIG = 16
LANES = SIG + DET * WIDE


def section_one_table():
    cols = np.arange(COLS)
    samples = 64 * (cols // WIDE) - HALO + cols % WIDE
    angle = 2.0 * np.pi * ((np.arange(LEN)[:, None] * samples[None, :]) % LEN) / LEN
    cos = np.cos(angle).reshape(LEN, NCHUNK, CHUNK)
    sin = np.sin(angle).reshape(LEN, NCHUNK, CHUNK)
    both = np.concatenate([cos, sin], axis=2)
    return np.ascontiguousarray(np.transpose(both, (1, 0, 2))).astype(ml_dtypes.bfloat16)


def last_section_table():
    table = np.zeros((ZS, 2, 2, ROWS, 2, 8, 8, 2))
    z = np.arange(ZS)[:, None, None, None]
    r = np.arange(ROWS)[None, :, None, None]
    m = np.arange(8)[None, None, :, None]
    h = np.arange(8)[None, None, None, :]
    angle = 2.0 * np.pi * (((8 * z + r) * (8 * m + h)) % 64) / 64
    for ql in range(2):
        table[:, ql, 0, :, 0, :, :, ql] = np.cos(angle)
        table[:, ql, 1, :, 0, :, :, ql] = -np.sin(angle)
        table[:, ql, 0, :, 1, :, :, ql] = np.sin(angle)
        table[:, ql, 1, :, 1, :, :, ql] = np.cos(angle)
    return table.reshape(256, 256).astype(ml_dtypes.bfloat16)


def unit_circle(turns):
    turns = turns & (FULL - 1)
    quarter = (turns + FULL // 8) >> 18
    x = (turns - (quarter << 18)).astype(F32) * (2.0 * math.pi / FULL)
    x2 = x * x
    s = x * (1.0 + x2 * (-1.0 / 6 + x2 * (1.0 / 120 + x2 * (-1.0 / 5040 + x2 * (1.0 / 362880)))))
    c = 1.0 + x2 * (-0.5 + x2 * (1.0 / 24 + x2 * (-1.0 / 720 + x2 * (1.0 / 40320))))
    odd = (quarter & 1) == 1
    cos = jnp.where(odd, s, c)
    sin = jnp.where(odd, c, s)
    cos = jnp.where(((quarter + 1) & 2) != 0, -cos, cos)
    sin = jnp.where((quarter & 2) != 0, -sin, sin)
    return cos, sin


def dft_four(a, b, c, d):
    sr, si = a[0] + c[0], a[1] + c[1]
    dr, di = a[0] - c[0], a[1] - c[1]
    tr, ti = b[0] + d[0], b[1] + d[1]
    er, ei = b[0] - d[0], b[1] - d[1]
    return (
        (sr + tr, si + ti),
        (dr - ei, di + er),
        (sr - tr, si - ti),
        (dr + ei, di - er),
    )


def dft_sixteen(cells):
    first = [dft_four(*[cells[4 * a + b] for a in range(4)]) for b in range(4)]
    out = [None] * 16
    for k0 in range(4):
        column = []
        for b in range(4):
            xr, xi = first[b][k0]
            turn = (b * k0) % 16
            if turn:
                wr = math.cos(2 * math.pi * turn / 16)
                wi = math.sin(2 * math.pi * turn / 16)
                xr, xi = xr * wr - xi * wi, xr * wi + xi * wr
            column.append((xr, xi))
        for k1, value in enumerate(dft_four(*column)):
            out[k0 + 4 * k1] = value
    return out


def split_two(x):
    high = x.astype(BF16).astype(F32)
    return high, x - high


def kernel(
    tmpl_hbm, strain_hbm, psd_hbm, ant, delay, tab_hbm, last_hbm,
    sky_out, peak_out,
    tmpl_v, strain_v, psd_v, tab_v, last_v, prod_v, twist_v, turn_v, turn2_v,
    send_xy, recv_xy, send_z, recv_z, fin_v, pk_v, send_r, recv_r, send_p, recv_p,
    load_sem, tab_sem, s_send, s_recv, xy_send, xy_recv, z_send, z_recv, r_send, r_recv, p_send, p_recv,
):
    t = lax.axis_index("tmpl")
    g = lax.axis_index("det")
    cell = lax.div(t, ZS)
    z = lax.rem(t, ZS)

    det_ids = [{"tmpl": t, "det": lax.rem(g + k, GROUPS)} for k in range(1, GROUPS)]
    cell_to = [lax.rem(cell + k, CELLS) for k in range(1, CELLS)]
    xy_ids = [{"tmpl": c * ZS + z, "det": g} for c in cell_to]
    z_to = [lax.rem(z + k, ZS) for k in range(1, ZS)]
    z_ids = [{"tmpl": cell * ZS + k, "det": g} for k in z_to]

    barrier = pltpu.get_barrier_semaphore()
    for who in det_ids + xy_ids + z_ids:
        pl.semaphore_signal(barrier, inc=1, device_id=who, device_id_type=MESH)

    loads = [
        pltpu.make_async_copy(strain_hbm, strain_v.at[g], load_sem.at[0]),
        pltpu.make_async_copy(tmpl_hbm, tmpl_v, load_sem.at[1]),
        pltpu.make_async_copy(psd_hbm, psd_v, load_sem.at[2]),
        pltpu.make_async_copy(last_hbm, last_v, load_sem.at[3]),
    ]
    tab_loads = [pltpu.make_async_copy(tab_hbm.at[n], tab_v.at[n], tab_sem.at[n]) for n in range(NCHUNK)]
    for copy in loads + tab_loads:
        copy.start()

    pl.semaphore_wait(barrier, len(det_ids) + len(xy_ids) + len(z_ids))

    s_copies = [
        pltpu.make_async_remote_copy(
            src_ref=strain_hbm, dst_ref=strain_v.at[g], send_sem=s_send.at[k], recv_sem=s_recv.at[k],
            device_id=det_ids[k], device_id_type=MESH,
        )
        for k in range(GROUPS - 1)
    ]
    for copy in s_copies:
        copy.start()

    row = lax.broadcasted_iota(jnp.int32, (ROWS, COLS), 0)
    col = lax.broadcasted_iota(jnp.int32, (ROWS, COLS), 1)
    sample = col - 2 * HALO * ((col * 52429) >> 22) - HALO
    cos, sin = unit_circle((t * ROWS + row) * sample)
    turn_v[0] = cos
    turn_v[1] = sin
    row = lax.broadcasted_iota(jnp.int32, (ROWS, 128), 0)
    for q in range(16):
        cos, sin = unit_circle((z * ROWS + row) * (q * LEN))
        turn2_v[0, q] = cos
        turn2_v[1, q] = sin

    for copy in loads[1:3]:
        copy.wait()
    both = tmpl_v[...].astype(F32)
    tr, ti = both[:ROWS], both[ROWS:]
    square = tr * tr + ti * ti
    parts = [
        split_two(jnp.sum(square * psd_v[ROWS * d : ROWS * d + ROWS, :], axis=1, keepdims=True))
        for d in range(DET)
    ]
    blank = jnp.zeros((ROWS, SIG - DET), F32)
    sig = [jnp.concatenate([parts[d][c] for d in range(DET)] + [blank], axis=1) for c in range(2)]

    loads[0].wait()
    for copy in s_copies:
        copy.wait_recv()
    for piece in range(GROUPS):
        lanes = slice(CHUNK * piece, CHUNK * piece + CHUNK)
        data = strain_v[piece].astype(F32)
        trl, til = tr[:, lanes], ti[:, lanes]
        real, imag = [], []
        for d in range(DET):
            dr = data[ROWS * d : ROWS * d + ROWS]
            di = data[ROWS * (DET + d) : ROWS * (DET + d) + ROWS]
            weight = psd_v[ROWS * d : ROWS * d + ROWS, lanes]
            real.append((trl * dr + til * di) * weight)
            imag.append((trl * di - til * dr) * weight)
        prod_v[:, lanes] = jnp.concatenate(real + imag, axis=0).astype(BF16)

    half = DET * ROWS
    product = prod_v[...]
    for n in range(NCHUNK):
        tab_loads[n].wait()
        out = jnp.dot(product, tab_v[n], preferred_element_type=F32)
        sec_r = out[:half, :CHUNK] - out[half:, CHUNK:]
        sec_i = out[:half, CHUNK:] + out[half:, :CHUNK]
        lanes = slice(CHUNK * n, CHUNK * n + CHUNK)
        cos, sin = turn_v[0, :, lanes], turn_v[1, :, lanes]
        for d in range(DET):
            rows = slice(ROWS * d, ROWS * d + ROWS)
            twist_v[0, rows, lanes] = sec_r[rows] * cos - sec_i[rows] * sin
            twist_v[1, rows, lanes] = sec_r[rows] * sin + sec_i[rows] * cos

    for c in range(CELLS):
        lanes = slice(WIDE * c, WIDE * c + WIDE)
        block = jnp.concatenate(
            [
                jnp.concatenate(
                    [sig[i]] + [twist_v[i, ROWS * d : ROWS * d + ROWS, lanes] for d in range(DET)], axis=1
                )
                for i in range(2)
            ],
            axis=0,
        ).astype(BF16)
        send_xy[0, c] = block[:, :128]
        send_xy[1, c] = block[:, 128:]

    xy_copies = []
    for part in range(2):
        copies = [
            pltpu.make_async_remote_copy(
                src_ref=send_xy.at[part, cell_to[k]], dst_ref=recv_xy.at[part, cell],
                send_sem=xy_send.at[part, k], recv_sem=xy_recv.at[part, k],
                device_id=xy_ids[k], device_id_type=MESH,
            )
            for k in range(CELLS - 1)
        ]
        for copy in copies:
            copy.start()
        xy_copies.append(copies)
        recv_xy[part, cell] = send_xy[part, cell]

    lane = lax.broadcasted_iota(jnp.int32, (ROWS, 128), 1)
    z_copies = []
    for part in range(2):
        for copy in xy_copies[part]:
            copy.wait_recv()
        cells = []
        for c in range(CELLS):
            value = recv_xy[part, c].astype(F32)
            cells.append((value[:ROWS], value[ROWS:]))
        bins = dft_sixteen(cells)
        if part == 0:
            high, low = split_two(bins[0][0] + bins[0][1])
        for q in range(16):
            xr, xi = bins[q]
            cos, sin = turn2_v[0, q], turn2_v[1, q]
            yr, yi = xr * cos - xi * sin, xr * sin + xi * cos
            if part == 0:
                yr = jnp.where(lane < SIG, high, yr)
                yi = jnp.where(lane < SIG, low, yi)
            send_z[part, q] = jnp.concatenate([yr, yi], axis=0).astype(BF16)
        copies = [
            pltpu.make_async_remote_copy(
                src_ref=send_z.at[part, pl.ds(2 * z_to[k], 2)], dst_ref=recv_z.at[part, z],
                send_sem=z_send.at[part, k], recv_sem=z_recv.at[part, k],
                device_id=z_ids[k], device_id_type=MESH,
            )
            for k in range(ZS - 1)
        ]
        for copy in copies:
            copy.start()
        z_copies.append(copies)
        recv_z[part, z] = send_z[part, pl.ds(2 * z, 2)]

    scales = None
    for part in range(2):
        for copy in z_copies[part]:
            copy.wait_recv()
        got = recv_z[part].reshape(256, 128)
        if part == 0:
            halves = recv_z[part, :, 0].astype(F32)
            total = jnp.sum(jnp.sum(halves, axis=0), axis=0, keepdims=True)
            scales = [1.0 / jnp.sqrt(total[:, d : d + 1]) for d in range(DET)]
        out = lax.dot_general(got, last_v[...] if part else _wait_load(loads[3], last_v), (((0,), (0,)), ((), ())), preferred_element_type=F32)
        for d in range(DET):
            low_row = max(SIG + WIDE * d, 128 * part)
            high_row = min(SIG + WIDE * (d + 1), 128 * part + 128)
            if low_row < high_row:
                block = out[low_row - 128 * part : high_row - 128 * part]
                fin_v[0, low_row:high_row, :] = block[:, :128] * scales[d]
                fin_v[1, low_row:high_row, :] = block[:, 128:] * scales[d]

    def visit(s, best):
        sum_r = sum_i = None
        for d in range(DET):
            rows = pl.ds(SIG + WIDE * d + HALO + delay[d, s], 64)
            gain = ant[d, s]
            real = gain * fin_v[0, rows, :]
            imag = gain * fin_v[1, rows, :]
            sum_r = real if sum_r is None else sum_r + real
            sum_i = imag if sum_i is None else sum_i + imag
        power = sum_r * sum_r + sum_i * sum_i
        pk_v[s] = jnp.max(power.reshape(8, 8, 128), axis=0)
        return jnp.maximum(best, power)

    best = lax.fori_loop(0, SKY, visit, jnp.zeros((64, 128), F32))

    tops = jnp.max(pk_v[...], axis=1)
    tops = jnp.max(jnp.transpose(tops), axis=0, keepdims=True)
    tops = jnp.concatenate([tops, jnp.zeros((1, 128 - SKY), F32)], axis=1)
    tops = jnp.broadcast_to(tops, (8, 128))
    for k in range(ZS):
        send_r[k, :8] = best[8 * k : 8 * k + 8]
        send_r[k, 8:] = tops
    r_copies = [
        pltpu.make_async_remote_copy(
            src_ref=send_r.at[z_to[k]], dst_ref=recv_r.at[z], send_sem=r_send.at[k], recv_sem=r_recv.at[k],
            device_id=z_ids[k], device_id_type=MESH,
        )
        for k in range(ZS - 1)
    ]
    for copy in r_copies:
        copy.start()
    recv_r[z] = send_r[z]
    for copy in r_copies:
        copy.wait_recv()
    tops = jnp.max(recv_r[:, 8:, :], axis=0)
    send_p[...] = tops
    p_copies = [
        pltpu.make_async_remote_copy(
            src_ref=send_p, dst_ref=recv_p.at[cell], send_sem=p_send.at[k], recv_sem=p_recv.at[k],
            device_id=xy_ids[k], device_id_type=MESH,
        )
        for k in range(CELLS - 1)
    ]
    for copy in p_copies:
        copy.start()
    recv_p[cell] = tops

    lane = lax.broadcasted_iota(jnp.int32, (8, 128), 1)
    owner = (lane >> 1) & 7
    for m in range(8):
        index = 16 * m + 2 * (lane >> 4) + (lane & 1)
        acc = jnp.zeros((8, 128), F32)
        for k in range(ZS):
            moved = jnp.take_along_axis(recv_r[k, :8], index, axis=1, mode="promise_in_bounds")
            acc = jnp.where(owner == k, moved, acc)
        sky_out[:, 128 * m : 128 * m + 128] = acc

    for copy in p_copies:
        copy.wait_recv()
    tops = jnp.max(recv_p[...], axis=0)
    peak_out[...] = tops[:1, :SKY]

    for copy in s_copies + xy_copies[0] + xy_copies[1] + z_copies[0] + z_copies[1] + r_copies + p_copies:
        copy.wait_send()


def _wait_load(copy, ref):
    copy.wait()
    return ref[...]


def shards(templates, strain, inverse_psd, antenna, delays):
    tab = jnp.asarray(section_one_table())
    last = jnp.asarray(last_section_table())
    any_spec = pl.BlockSpec(memory_space=pl.ANY)
    smem = pl.BlockSpec(memory_space=pltpu.SMEM)
    vmem = pl.BlockSpec(memory_space=pltpu.VMEM)
    dma = pltpu.SemaphoreType.DMA
    sky, peak = pl.pallas_call(
        kernel,
        out_shape=(
            jax.ShapeDtypeStruct((8, LEN), F32),
            jax.ShapeDtypeStruct((1, SKY), F32),
        ),
        in_specs=[any_spec, any_spec, any_spec, smem, smem, any_spec, any_spec],
        out_specs=(vmem, vmem),
        scratch_shapes=[
            pltpu.VMEM((16, LEN), BF16),
            pltpu.VMEM((GROUPS, 48, CHUNK), BF16),
            pltpu.VMEM((24, LEN), F32),
            pltpu.VMEM((NCHUNK, LEN, 2 * CHUNK), BF16),
            pltpu.VMEM((256, 256), BF16),
            pltpu.VMEM((48, LEN), BF16),
            pltpu.VMEM((2, 24, COLS), F32),
            pltpu.VMEM((2, ROWS, COLS), F32),
            pltpu.VMEM((2, 16, ROWS, 128), F32),
            pltpu.VMEM((2, CELLS, 16, 128), BF16),
            pltpu.VMEM((2, CELLS, 16, 128), BF16),
            pltpu.VMEM((2, 16, 16, 128), BF16),
            pltpu.VMEM((2, ZS, 2, 16, 128), BF16),
            pltpu.VMEM((2, 256, 128), F32),
            pltpu.VMEM((SKY, 8, 128), F32),
            pltpu.VMEM((ZS, 16, 128), F32),
            pltpu.VMEM((ZS, 16, 128), F32),
            pltpu.VMEM((8, 128), F32),
            pltpu.VMEM((CELLS, 8, 128), F32),
            dma((4,)), dma((NCHUNK,)),
            dma((GROUPS - 1,)), dma((GROUPS - 1,)),
            dma((2, CELLS - 1)), dma((2, CELLS - 1)),
            dma((2, ZS - 1)), dma((2, ZS - 1)),
            dma((ZS - 1,)), dma((ZS - 1,)),
            dma((CELLS - 1,)), dma((CELLS - 1,)),
        ],
        compiler_params=pltpu.CompilerParams(
            collective_id=0, has_side_effects=True, vmem_limit_bytes=40 * 1024 * 1024
        ),
        cost_estimate=pl.CostEstimate(flops=400_000_000, bytes_accessed=6_000_000, transcendentals=0),
    )(
        templates.reshape(16, LEN),
        strain.reshape(48, CHUNK),
        inverse_psd.reshape(24, LEN),
        antenna,
        delays,
        tab,
        last,
    )
    return (sky[None], peak)


def solution(mesh):
    return jax.shard_map(
        shards,
        mesh=mesh,
        in_specs=(
            P(None, "det", "tmpl", None),
            P(None, None, "tmpl", "det"),
            P(None, "tmpl", None),
            P(),
            P(),
        ),
        out_specs=(P("det", "tmpl", None), P("det", None)),
        check_vma=False,
    )
```

time: 1970 us -> 61.6 us (0.03)
  the two profiles are of different devices: /device:TPU:32 before, /device:TPU:1 now
where the time goes in v1:
time: 61.6 us; the launch traced here: 61.2 us
  Pallas kernels  52.3 us (85%)
  local copies, waits for them, and re-layouts  8.26 us (13%)
  between operations  0.65 us (1%)
    pallas_call x1, Pallas kernels, shards(): pl.pallas_call(kernel, out_shape=(jax.ShapeDtypeStruct((8, LEN), F32), ja...  52.3 us
    unnamed x16, local copies, waits for them, and re-layouts  8.26 us

profile of v1, /device:TPU:1, one launch (start us, length us, event | category | flops | bytes accessed | tf_op | source)
XLA Modules:
  0.0 61.2 jit_solution(10880927010106295107)
XLA Ops:
  0.6 0.0 copy-start
  0.6 2.5 %copy-done = bf16[5,1024,512]{2,1,0:T(8,128)(2,1)S(1)} copy-done((bf16[5,1024,512]{2,1,0:T(8,128)(2,1)S(1)}, bf16[5,1024,512]{2,1,0:T(8,128)(2,1)}, u32[]{:S(2)}) %copy-start) | copy-done | bytes 5242904
  3.1 0.0 copy-start.1
  3.1 0.9 %copy-done.1 = bf16[256,256]{1,0:T(8,128)(2,1)S(1)} copy-done((bf16[256,256]{1,0:T(8,128)(2,1)S(1)}, bf16[256,256]{1,0:T(8,128)(2,1)}, u32[]{:S(2)}) %copy-start.1) | copy-done | bytes 131096
  4.0 0.0 copy-start.2
  4.0 0.9 %copy-done.2 = f32[3,8,1024]{2,1,0:T(8,128)S(1)} copy-done((f32[3,8,1024]{2,1,0:T(8,128)S(1)}, f32[3,8,1024]{2,1,0:T(8,128)}, u32[]{:S(2)}) %copy-start.2) | copy-done | bytes 98328
  4.9 0.0 copy-start.3
  4.9 0.8 %copy-done.3 = bf16[2,1,8,1024]{3,2,1,0:T(8,128)(2,1)S(1)} copy-done((bf16[2,1,8,1024]{3,2,1,0:T(8,128)(2,1)S(1)}, bf16[2,1,8,1024]{3,2,1,0:T(8,128)(2,1)}, u32[]{:S(2)}) %copy-start.3) | copy-done | bytes 32792
  5.7 0.0 copy-start.4
  5.7 0.7 %copy-done.4 = bf16[2,3,8,256]{3,2,1,0:T(8,128)(2,1)S(1)} copy-done((bf16[2,3,8,256]{3,2,1,0:T(8,128)(2,1)S(1)}, bf16[2,3,8,256]{3,2,1,0:T(8,128)(2,1)}, u32[]{:S(2)}) %copy-start.4) | copy-done | bytes 24600
  6.4 0.0 copy-start.5
  6.4 0.7 %copy-done.5 = f32[3,64]{1,0:T(4,128)S(1)} copy-done((f32[3,64]{1,0:T(4,128)S(1)}, f32[3,64]{1,0:T(4,128)}, u32[]{:S(2)}) %copy-start.5) | copy-done | bytes 792
  7.1 0.0 copy-start.6
  7.1 0.7 %copy-done.6 = s32[3,64]{1,0:T(4,128)S(1)} copy-done((s32[3,64]{1,0:T(4,128)S(1)}, s32[3,64]{1,0:T(4,128)}, u32[]{:S(2)}) %copy-start.6) | copy-done | bytes 792
  7.8 52.3 %shard_map.86 = (f32[8,1024]{1,0:T(8,128)S(1)}, f32[1,64]{1,0:T(1,128)S(1)}) custom-call(bf16[16,1024]{1,0:T(8,128)(2,1)S(1)} %bitcast.5, bf16[48,256]{1,0:T(8,128)(2,1)S(1)} %bitcast.7, f32[24,1024]{1,0:T(8,128)S(1)} %bitcast.4, f32[3,64]{1,0:T(4,128)S(1)} %copy-done.5, s32[3,64]{1,0:T(4,128)S(1)} %copy-done.6, bf16[5,1024,512]{2,1,0:T(8,128)(2,1)S(1)} %copy-done, ...), custom_call_target="tpu_custom_call" | custom-call | flops 400000000 | bytes 6000000 | tf_op jit(solution)/shard_map/pallas_call | solution.py:365
  60.1 0.6 %copy.11 = f32[1,8,1024]{2,1,0:T(8,128)} copy(f32[1,8,1024]{2,1,0:T(8,128)S(1)} %bitcast.6) | data formatting | bytes 65536
  60.7 0.5 copy.12
Async XLA Ops:
  0.6 2.5 %copy-start = (bf16[5,1024,512]{2,1,0:T(8,128)(2,1)S(1)}, bf16[5,1024,512]{2,1,0:T(8,128)(2,1)}, u32[]{:S(2)}) copy-start(bf16[5,1024,512]{2,1,0:T(8,128)(2,1)} %constant.4.clone.tab_hbm) | copy-start | bytes 15728644
  3.1 0.9 %copy-start.1 = (bf16[256,256]{1,0:T(8,128)(2,1)S(1)}, bf16[256,256]{1,0:T(8,128)(2,1)}, u32[]{:S(2)}) copy-start(bf16[256,256]{1,0:T(8,128)(2,1)} %constant.5.clone.last_hbm) | copy-start | bytes 393220
  4.0 0.9 %copy-start.2 = (f32[3,8,1024]{2,1,0:T(8,128)S(1)}, f32[3,8,1024]{2,1,0:T(8,128)}, u32[]{:S(2)}) copy-start(f32[3,8,1024]{2,1,0:T(8,128)} %param.9) | copy-start | bytes 294916
  4.9 0.8 %copy-start.3 = (bf16[2,1,8,1024]{3,2,1,0:T(8,128)(2,1)S(1)}, bf16[2,1,8,1024]{3,2,1,0:T(8,128)(2,1)}, u32[]{:S(2)}) copy-start(bf16[2,1,8,1024]{3,2,1,0:T(8,128)(2,1)} %param.7) | copy-start | bytes 98308
  5.7 0.7 %copy-start.4 = (bf16[2,3,8,256]{3,2,1,0:T(8,128)(2,1)S(1)}, bf16[2,3,8,256]{3,2,1,0:T(8,128)(2,1)}, u32[]{:S(2)}) copy-start(bf16[2,3,8,256]{3,2,1,0:T(8,128)(2,1)} %param.8) | copy-start | bytes 73732
  6.4 0.7 %copy-start.5 = (f32[3,64]{1,0:T(4,128)S(1)}, f32[3,64]{1,0:T(4,128)}, u32[]{:S(2)}) copy-start(f32[3,64]{1,0:T(4,128)} %ant.1) | copy-start | bytes 2308
  7.1 0.7 %copy-start.6 = (s32[3,64]{1,0:T(4,128)S(1)}, s32[3,64]{1,0:T(4,128)}, u32[]{:S(2)}) copy-start(s32[3,64]{1,0:T(4,128)} %delay.1) | copy-start | bytes 2308

commit v2 on v1

--- a/solution.py
+++ b/solution.py
@@ -107,48 +107,88 @@
 
 
 def kernel(
-    tmpl_hbm, strain_hbm, psd_hbm, ant, delay, tab_hbm, last_hbm,
+    tmpl_hbm, strain_hbm, psd_hbm, ant_hbm, delay_hbm, tab_hbm, last_hbm,
     sky_out, peak_out,
-    tmpl_v, strain_v, psd_v, tab_v, last_v, prod_v, twist_v, turn_v, turn2_v,
+    ant, delay, tmpl_v, strain_v, psd_v, tab_v, last_v, acc_v, twist_v, turn_v, turn2_v,
     send_xy, recv_xy, send_z, recv_z, fin_v, pk_v, send_r, recv_r, send_p, recv_p,
-    load_sem, tab_sem, s_send, s_recv, xy_send, xy_recv, z_send, z_recv, r_send, r_recv, p_send, p_recv,
+    load_sem, tab_sem, s_send, s_recv, relay_v, relay_send, relay_recv, ready_xy, ready_z, go_xy, go_z, xy_send, xy_recv, z_send, z_recv, r_send, r_recv, p_send, p_recv,
 ):
     t = lax.axis_index("tmpl")
     g = lax.axis_index("det")
     cell = lax.div(t, ZS)
     z = lax.rem(t, ZS)
 
-    det_ids = [{"tmpl": t, "det": lax.rem(g + k, GROUPS)} for k in range(1, GROUPS)]
+    late = lax.div(g, 2)
+    near_z = z < ZS // 2
+    core_g = g + 1 - 2 * lax.rem(g, 2)
+    far_g = lax.rem(g + 2, GROUPS)
+    diag_g = lax.rem(core_g + 2, GROUPS)
+    core_id = {"tmpl": t, "det": core_g}
+    far_id = {"tmpl": t, "det": far_g}
     cell_to = [lax.rem(cell + k, CELLS) for k in range(1, CELLS)]
     xy_ids = [{"tmpl": c * ZS + z, "det": g} for c in cell_to]
     z_to = [lax.rem(z + k, ZS) for k in range(1, ZS)]
     z_ids = [{"tmpl": cell * ZS + k, "det": g} for k in z_to]
 
+    def signal(sem, who):
+        pl.semaphore_signal(sem, inc=1, device_id=who, device_id_type=MESH)
+
     barrier = pltpu.get_barrier_semaphore()
-    for who in det_ids + xy_ids + z_ids:
-        pl.semaphore_signal(barrier, inc=1, device_id=who, device_id_type=MESH)
+
+    @pl.when(late == 0)
+    def _():
+        @pl.when(near_z)
+        def _():
+            signal(barrier, far_id)
+            signal(barrier, {"tmpl": t + ZS // 2, "det": far_g})
+
+    signal(barrier, core_id)
+
+    @pl.when(late == 0)
+    def _():
+        for who in z_ids + xy_ids:
+            signal(barrier, who)
 
     loads = [
         pltpu.make_async_copy(strain_hbm, strain_v.at[g], load_sem.at[0]),
         pltpu.make_async_copy(tmpl_hbm, tmpl_v, load_sem.at[1]),
         pltpu.make_async_copy(psd_hbm, psd_v, load_sem.at[2]),
         pltpu.make_async_copy(last_hbm, last_v, load_sem.at[3]),
+        pltpu.make_async_copy(ant_hbm, ant, load_sem.at[4]),
+        pltpu.make_async_copy(delay_hbm, delay, load_sem.at[5]),
     ]
     tab_loads = [pltpu.make_async_copy(tab_hbm.at[n], tab_v.at[n], tab_sem.at[n]) for n in range(NCHUNK)]
     for copy in loads + tab_loads:
         copy.start()
 
-    pl.semaphore_wait(barrier, len(det_ids) + len(xy_ids) + len(z_ids))
-
-    s_copies = [
-        pltpu.make_async_remote_copy(
-            src_ref=strain_hbm, dst_ref=strain_v.at[g], send_sem=s_send.at[k], recv_sem=s_recv.at[k],
-            device_id=det_ids[k], device_id_type=MESH,
+    def remote(source, target, send, recv, who):
+        return pltpu.make_async_remote_copy(
+            src_ref=source, dst_ref=target, send_sem=send, recv_sem=recv, device_id=who, device_id_type=MESH
         )
-        for k in range(GROUPS - 1)
-    ]
-    for copy in s_copies:
-        copy.start()
+
+    to_core = remote(strain_hbm, strain_v.at[g], s_send.at[0], s_recv.at[0], core_id)
+    to_far = remote(strain_hbm, strain_v.at[g], s_send.at[1], s_recv.at[1], far_id)
+    to_relay = remote(strain_hbm, relay_v, s_send.at[1], relay_recv, {"tmpl": t - ZS // 2, "det": far_g})
+    relayed = remote(relay_v, strain_v.at[far_g], relay_send, s_recv.at[1], {"tmpl": t + ZS // 2, "det": g})
+    handed_on = remote(strain_v.at[far_g], strain_v.at[far_g], s_send.at[2], s_recv.at[2], core_id)
+
+    @pl.when(late == 0)
+    def _():
+        pl.semaphore_wait(barrier, 1 + (ZS - 1) + (CELLS - 1))
+
+    @pl.when(late == 1)
+    def _():
+        pl.semaphore_wait(barrier, 2)
+
+        @pl.when(near_z)
+        def _():
+            to_far.start()
+
+        @pl.when(jnp.logical_not(near_z))
+        def _():
+            to_relay.start()
+
+    to_core.start()
 
     row = lax.broadcasted_iota(jnp.int32, (ROWS, COLS), 0)
     col = lax.broadcasted_iota(jnp.int32, (ROWS, COLS), 1)
@@ -174,13 +214,38 @@
     blank = jnp.zeros((ROWS, SIG - DET), F32)
     sig = [jnp.concatenate([parts[d][c] for d in range(DET)] + [blank], axis=1) for c in range(2)]
 
-    loads[0].wait()
-    for copy in s_copies:
-        copy.wait_recv()
-    for piece in range(GROUPS):
-        lanes = slice(CHUNK * piece, CHUNK * piece + CHUNK)
+    half = DET * ROWS
+    for order, piece in enumerate([g, core_g, far_g, diag_g]):
+        if order == 0:
+            loads[0].wait()
+            for copy in tab_loads:
+                copy.wait()
+        elif order == 1:
+            to_core.wait_recv()
+        elif order == 2:
+
+            @pl.when(jnp.logical_and(late == 0, near_z))
+            def _():
+                to_relay.wait_recv()
+                relayed.start()
+
+            to_far.wait_recv()
+            handed_on.start()
+
+            @pl.when(late == 0)
+            def _():
+                to_far.start()
+                for who in xy_ids:
+                    signal(ready_xy, who)
+                for who in z_ids:
+                    signal(ready_z, who)
+
+        else:
+            handed_on.wait_recv()
+        lanes = pl.ds(pl.multiple_of(CHUNK * piece, CHUNK), CHUNK)
         data = strain_v[piece].astype(F32)
-        trl, til = tr[:, lanes], ti[:, lanes]
+        both = tmpl_v[:, lanes].astype(F32)
+        trl, til = both[:ROWS], both[ROWS:]
         real, imag = [], []
         for d in range(DET):
             dr = data[ROWS * d : ROWS * d + ROWS]
@@ -188,21 +253,22 @@
             weight = psd_v[ROWS * d : ROWS * d + ROWS, lanes]
             real.append((trl * dr + til * di) * weight)
             imag.append((trl * di - til * dr) * weight)
-        prod_v[:, lanes] = jnp.concatenate(real + imag, axis=0).astype(BF16)
-
-    half = DET * ROWS
-    product = prod_v[...]
-    for n in range(NCHUNK):
-        tab_loads[n].wait()
-        out = jnp.dot(product, tab_v[n], preferred_element_type=F32)
-        sec_r = out[:half, :CHUNK] - out[half:, CHUNK:]
-        sec_i = out[:half, CHUNK:] + out[half:, :CHUNK]
-        lanes = slice(CHUNK * n, CHUNK * n + CHUNK)
-        cos, sin = turn_v[0, :, lanes], turn_v[1, :, lanes]
-        for d in range(DET):
-            rows = slice(ROWS * d, ROWS * d + ROWS)
-            twist_v[0, rows, lanes] = sec_r[rows] * cos - sec_i[rows] * sin
-            twist_v[1, rows, lanes] = sec_r[rows] * sin + sec_i[rows] * cos
+        product = jnp.concatenate(real + imag, axis=0).astype(BF16)
+        for n in range(NCHUNK):
+            out = jnp.dot(product, tab_v[n, lanes, :], preferred_element_type=F32)
+            if order:
+                out = out + acc_v[n]
+            if order < GROUPS - 1:
+                acc_v[n] = out
+                continue
+            sec_r = out[:half, :CHUNK] - out[half:, CHUNK:]
+            sec_i = out[:half, CHUNK:] + out[half:, :CHUNK]
+            cols = slice(CHUNK * n, CHUNK * n + CHUNK)
+            cos, sin = turn_v[0, :, cols], turn_v[1, :, cols]
+            for d in range(DET):
+                rows = slice(ROWS * d, ROWS * d + ROWS)
+                twist_v[0, rows, cols] = sec_r[rows] * cos - sec_i[rows] * sin
+                twist_v[1, rows, cols] = sec_r[rows] * sin + sec_i[rows] * cos
 
     for c in range(CELLS):
         lanes = slice(WIDE * c, WIDE * c + WIDE)
@@ -217,6 +283,10 @@
         ).astype(BF16)
         send_xy[0, c] = block[:, :128]
         send_xy[1, c] = block[:, 128:]
+
+    @pl.when(late == 1)
+    def _():
+        pl.semaphore_wait(go_xy, 1)
 
     xy_copies = []
     for part in range(2):
@@ -232,6 +302,13 @@
             copy.start()
         xy_copies.append(copies)
         recv_xy[part, cell] = send_xy[part, cell]
+
+    @pl.when(late == 0)
+    def _():
+        pl.semaphore_wait(ready_xy, CELLS - 1)
+        signal(go_xy, far_id)
+        pl.semaphore_wait(ready_z, ZS - 1)
+        signal(go_z, far_id)
 
     lane = lax.broadcasted_iota(jnp.int32, (ROWS, 128), 1)
     z_copies = []
@@ -261,6 +338,12 @@
             )
             for k in range(ZS - 1)
         ]
+        if part == 0:
+
+            @pl.when(late == 1)
+            def _():
+                pl.semaphore_wait(go_z, 1)
+
         for copy in copies:
             copy.start()
         z_copies.append(copies)
@@ -297,6 +380,8 @@
         pk_v[s] = jnp.max(power.reshape(8, 8, 128), axis=0)
         return jnp.maximum(best, power)
 
+    loads[4].wait()
+    loads[5].wait()
     best = lax.fori_loop(0, SKY, visit, jnp.zeros((64, 128), F32))
 
     tops = jnp.max(pk_v[...], axis=1)
@@ -346,7 +431,14 @@
     tops = jnp.max(recv_p[...], axis=0)
     peak_out[...] = tops[:1, :SKY]
 
-    for copy in s_copies + xy_copies[0] + xy_copies[1] + z_copies[0] + z_copies[1] + r_copies + p_copies:
+    for copy in (to_core, to_far, handed_on):
+        copy.wait_send()
+
+    @pl.when(jnp.logical_and(late == 0, near_z))
+    def _():
+        relayed.wait_send()
+
+    for copy in xy_copies[0] + xy_copies[1] + z_copies[0] + z_copies[1] + r_copies + p_copies:
         copy.wait_send()
 
 
@@ -358,25 +450,27 @@
 def shards(templates, strain, inverse_psd, antenna, delays):
     tab = jnp.asarray(section_one_table())
     last = jnp.asarray(last_section_table())
-    any_spec = pl.BlockSpec(memory_space=pl.ANY)
-    smem = pl.BlockSpec(memory_space=pltpu.SMEM)
+    hbm = pl.BlockSpec(memory_space=pltpu.HBM)
     vmem = pl.BlockSpec(memory_space=pltpu.VMEM)
     dma = pltpu.SemaphoreType.DMA
+    regular = pltpu.SemaphoreType.REGULAR
     sky, peak = pl.pallas_call(
         kernel,
         out_shape=(
             jax.ShapeDtypeStruct((8, LEN), F32),
             jax.ShapeDtypeStruct((1, SKY), F32),
         ),
-        in_specs=[any_spec, any_spec, any_spec, smem, smem, any_spec, any_spec],
+        in_specs=[hbm] * 7,
         out_specs=(vmem, vmem),
         scratch_shapes=[
+            pltpu.SMEM((DET, SKY), F32),
+            pltpu.SMEM((DET, SKY), jnp.int32),
             pltpu.VMEM((16, LEN), BF16),
             pltpu.VMEM((GROUPS, 48, CHUNK), BF16),
             pltpu.VMEM((24, LEN), F32),
             pltpu.VMEM((NCHUNK, LEN, 2 * CHUNK), BF16),
             pltpu.VMEM((256, 256), BF16),
-            pltpu.VMEM((48, LEN), BF16),
+            pltpu.VMEM((NCHUNK, 48, 2 * CHUNK), F32),
             pltpu.VMEM((2, 24, COLS), F32),
             pltpu.VMEM((2, ROWS, COLS), F32),
             pltpu.VMEM((2, 16, ROWS, 128), F32),
@@ -390,15 +484,18 @@
             pltpu.VMEM((ZS, 16, 128), F32),
             pltpu.VMEM((8, 128), F32),
             pltpu.VMEM((CELLS, 8, 128), F32),
-            dma((4,)), dma((NCHUNK,)),
+            dma((6,)), dma((NCHUNK,)),
             dma((GROUPS - 1,)), dma((GROUPS - 1,)),
+            pltpu.VMEM((48, CHUNK), BF16),
+            dma, dma,
+            regular, regular, regular, regular,
             dma((2, CELLS - 1)), dma((2, CELLS - 1)),
             dma((2, ZS - 1)), dma((2, ZS - 1)),
             dma((ZS - 1,)), dma((ZS - 1,)),
             dma((CELLS - 1,)), dma((CELLS - 1,)),
         ],
         compiler_params=pltpu.CompilerParams(
-            collective_id=0, has_side_effects=True, vmem_limit_bytes=40 * 1024 * 1024
+            collective_id=0, has_side_effects=True, vmem_limit_bytes=60 * 1024 * 1024
         ),
         cost_estimate=pl.CostEstimate(flops=400_000_000, bytes_accessed=6_000_000, transcendentals=0),
     )(

time: 61.6 us -> 54.7 us (0.89)
  the two profiles are of different devices: /device:TPU:1 before, /device:TPU:480 now
where the time goes in v2:
time: 54.7 us; the launch traced here: 54.5 us
  Pallas kernels  51.3 us (94%)
  local copies, waits for them, and re-layouts  2.55 us (5%)
  between operations  0.64 us (1%)
    pallas_call x1, Pallas kernels, shards(): pl.pallas_call(kernel, out_shape=(jax.ShapeDtypeStruct((8, LEN), F32), ja...  51.3 us
    unnamed x2, local copies, waits for them, and re-layouts  2.55 us

profile of v2, /device:TPU:480, one launch (start us, length us, event | category | flops | bytes accessed | tf_op | source)
XLA Modules:
  0.0 54.5 jit_solution(8148267957178212318)
XLA Ops:
  0.6 51.3 %shard_map.86 = (f32[8,1024]{1,0:T(8,128)}, f32[1,64]{1,0:T(1,128)}) custom-call(bf16[16,1024]{1,0:T(8,128)(2,1)} %bitcast.5, bf16[48,256]{1,0:T(8,128)(2,1)} %bitcast.7, f32[24,1024]{1,0:T(8,128)} %bitcast.4, f32[3,64]{1,0:T(4,128)} %ant_hbm.1, s32[3,64]{1,0:T(4,128)} %delay_hbm.1, bf16[5,1024,512]{2,1,0:T(8,128)(2,1)} %constant.4.clone.tab_hbm, ...), custom_call_target="tpu_custom_call" | custom-call | flops 400000000 | bytes 6000000 | tf_op jit(solution)/shard_map/pallas_call | solution.py:457
  51.9 1.4 %copy.11 = f32[1,8,1024]{2,1,0:T(8,128)} copy(f32[1,8,1024]{2,1,0:T(8,128)} %bitcast.6) | data formatting | bytes 65536
  53.3 1.2 %copy.12 = f32[1,64]{1,0:T(1,128)} copy(f32[1,64]{1,0:T(1,128)} %get-tuple-element.9) | data formatting | bytes 512

commit v3 on v2

--- a/solution.py
+++ b/solution.py
@@ -101,6 +101,19 @@
     return out
 
 
+def z_far_first(z):
+    upper = z >= ZS // 2
+    low = jnp.where(upper, ZS - 1 - z, z)
+    alone = ZS - 1 - 2 * low
+    places = []
+    for j in range(ZS - 1):
+        step = low - lax.div(jnp.maximum(j - alone, 0), 2)
+        side = lax.rem(jnp.maximum(j - alone, 0), 2)
+        place = jnp.where(j < alone, ZS - 1 - j, low + step - 2 * step * side)
+        places.append(jnp.where(upper, ZS - 1 - place, place))
+    return places
+
+
 def split_two(x):
     high = x.astype(BF16).astype(F32)
     return high, x - high
@@ -111,7 +124,7 @@
     sky_out, peak_out,
     ant, delay, tmpl_v, strain_v, psd_v, tab_v, last_v, acc_v, twist_v, turn_v, turn2_v,
     send_xy, recv_xy, send_z, recv_z, fin_v, pk_v, send_r, recv_r, send_p, recv_p,
-    load_sem, tab_sem, s_send, s_recv, relay_v, relay_send, relay_recv, ready_xy, ready_z, go_xy, go_z, xy_send, xy_recv, z_send, z_recv, r_send, r_recv, p_send, p_recv,
+    load_sem, tab_sem, s_send, s_recv, relay_v, relay_send, relay_recv, hello, hello_relay, ready_xy, ready_z, go_xy, go_z, xy_send, xy_recv, z_send, z_recv, r_send, r_recv, p_send, p_recv,
 ):
     t = lax.axis_index("tmpl")
     g = lax.axis_index("det")
@@ -127,7 +140,7 @@
     far_id = {"tmpl": t, "det": far_g}
     cell_to = [lax.rem(cell + k, CELLS) for k in range(1, CELLS)]
     xy_ids = [{"tmpl": c * ZS + z, "det": g} for c in cell_to]
-    z_to = [lax.rem(z + k, ZS) for k in range(1, ZS)]
+    z_to = z_far_first(z)
     z_ids = [{"tmpl": cell * ZS + k, "det": g} for k in z_to]
 
     def signal(sem, who):
@@ -176,16 +189,23 @@
     def _():
         pl.semaphore_wait(barrier, 1 + (ZS - 1) + (CELLS - 1))
 
-    @pl.when(late == 1)
-    def _():
-        pl.semaphore_wait(barrier, 2)
-
         @pl.when(near_z)
         def _():
+            pl.semaphore_wait(hello_relay, 1)
+            signal(hello, {"tmpl": t + ZS // 2, "det": g})
+
+    @pl.when(late == 1)
+    def _():
+        pl.semaphore_wait(barrier, 2)
+
+        @pl.when(near_z)
+        def _():
+            signal(hello, far_id)
             to_far.start()
 
         @pl.when(jnp.logical_not(near_z))
         def _():
+            signal(hello_relay, {"tmpl": t - ZS // 2, "det": far_g})
             to_relay.start()
 
     to_core.start()
@@ -229,17 +249,17 @@
                 to_relay.wait_recv()
                 relayed.start()
 
-            to_far.wait_recv()
-            handed_on.start()
-
             @pl.when(late == 0)
             def _():
+                pl.semaphore_wait(hello, 1)
                 to_far.start()
                 for who in xy_ids:
                     signal(ready_xy, who)
                 for who in z_ids:
                     signal(ready_z, who)
 
+            to_far.wait_recv()
+            handed_on.start()
         else:
             handed_on.wait_recv()
         lanes = pl.ds(pl.multiple_of(CHUNK * piece, CHUNK), CHUNK)
@@ -333,7 +353,7 @@
         copies = [
             pltpu.make_async_remote_copy(
                 src_ref=send_z.at[part, pl.ds(2 * z_to[k], 2)], dst_ref=recv_z.at[part, z],
-                send_sem=z_send.at[part, k], recv_sem=z_recv.at[part, k],
+                send_sem=z_send.at[part, k], recv_sem=z_recv.at[part, z],
                 device_id=z_ids[k], device_id_type=MESH,
             )
             for k in range(ZS - 1)
@@ -351,8 +371,8 @@
 
     scales = None
     for part in range(2):
-        for copy in z_copies[part]:
-            copy.wait_recv()
+        for k in z_to:
+            pltpu.make_async_copy(recv_z.at[part, k], recv_z.at[part, k], z_recv.at[part, k]).wait()
         got = recv_z[part].reshape(256, 128)
         if part == 0:
             halves = recv_z[part, :, 0].astype(F32)
@@ -384,52 +404,44 @@
     loads[5].wait()
     best = lax.fori_loop(0, SKY, visit, jnp.zeros((64, 128), F32))
 
-    tops = jnp.max(pk_v[...], axis=1)
-    tops = jnp.max(jnp.transpose(tops), axis=0, keepdims=True)
-    tops = jnp.concatenate([tops, jnp.zeros((1, 128 - SKY), F32)], axis=1)
-    tops = jnp.broadcast_to(tops, (8, 128))
     for k in range(ZS):
-        send_r[k, :8] = best[8 * k : 8 * k + 8]
-        send_r[k, 8:] = tops
+        send_r[k] = best[8 * k : 8 * k + 8]
     r_copies = [
-        pltpu.make_async_remote_copy(
-            src_ref=send_r.at[z_to[k]], dst_ref=recv_r.at[z], send_sem=r_send.at[k], recv_sem=r_recv.at[k],
-            device_id=z_ids[k], device_id_type=MESH,
-        )
-        for k in range(ZS - 1)
+        remote(send_r.at[z_to[k]], recv_r.at[z], r_send.at[k], r_recv.at[z], z_ids[k]) for k in range(ZS - 1)
     ]
     for copy in r_copies:
         copy.start()
     recv_r[z] = send_r[z]
-    for copy in r_copies:
-        copy.wait_recv()
-    tops = jnp.max(recv_r[:, 8:, :], axis=0)
-    send_p[...] = tops
-    p_copies = [
-        pltpu.make_async_remote_copy(
-            src_ref=send_p, dst_ref=recv_p.at[cell], send_sem=p_send.at[k], recv_sem=p_recv.at[k],
-            device_id=xy_ids[k], device_id_type=MESH,
-        )
-        for k in range(CELLS - 1)
-    ]
-    for copy in p_copies:
-        copy.start()
-    recv_p[cell] = tops
-
+
+    tops = jnp.max(pk_v[...], axis=1)
+    tops = jnp.max(jnp.transpose(tops), axis=0, keepdims=True)
+    tops = jnp.concatenate([tops, jnp.zeros((1, 128 - SKY), F32)], axis=1)
+    send_p[...] = jnp.broadcast_to(tops, (8, 128))
+    others = CELLS * ZS - 1
+
+    def tell(k, carry):
+        who = lax.rem(t + k, CELLS * ZS)
+        remote(send_p.at[pl.ds(0, 1)], recv_p.at[pl.ds(t, 1)], p_send, p_recv, {"tmpl": who, "det": g}).start()
+        return carry
+
+    lax.fori_loop(1, CELLS * ZS, tell, 0)
+    recv_p[pl.ds(t, 1), :] = tops
+
+    for k in z_to:
+        pltpu.make_async_copy(recv_r.at[k], recv_r.at[k], r_recv.at[k]).wait()
     lane = lax.broadcasted_iota(jnp.int32, (8, 128), 1)
     owner = (lane >> 1) & 7
     for m in range(8):
         index = 16 * m + 2 * (lane >> 4) + (lane & 1)
         acc = jnp.zeros((8, 128), F32)
         for k in range(ZS):
-            moved = jnp.take_along_axis(recv_r[k, :8], index, axis=1, mode="promise_in_bounds")
+            moved = jnp.take_along_axis(recv_r[k], index, axis=1, mode="promise_in_bounds")
             acc = jnp.where(owner == k, moved, acc)
         sky_out[:, 128 * m : 128 * m + 128] = acc
 
-    for copy in p_copies:
-        copy.wait_recv()
-    tops = jnp.max(recv_p[...], axis=0)
-    peak_out[...] = tops[:1, :SKY]
+    rows = pl.ds(0, others)
+    pltpu.make_async_copy(recv_p.at[rows], recv_p.at[rows], p_recv).wait()
+    peak_out[...] = jnp.max(recv_p[...], axis=0, keepdims=True)[:, :SKY]
 
     for copy in (to_core, to_far, handed_on):
         copy.wait_send()
@@ -438,13 +450,22 @@
     def _():
         relayed.wait_send()
 
-    for copy in xy_copies[0] + xy_copies[1] + z_copies[0] + z_copies[1] + r_copies + p_copies:
+    for copy in xy_copies[0] + xy_copies[1] + z_copies[0] + z_copies[1] + r_copies:
         copy.wait_send()
+    pltpu.make_async_copy(recv_p.at[rows], recv_p.at[rows], p_send).wait()
 
 
 def _wait_load(copy, ref):
     copy.wait()
     return ref[...]
+
+
+def hand_over(sky_in, peak_in, sky_out, peak_out, sem):
+    copies = [pltpu.make_async_copy(sky_in, sky_out, sem.at[0]), pltpu.make_async_copy(peak_in, peak_out, sem.at[1])]
+    for copy in copies:
+        copy.start()
+    for copy in copies:
+        copy.wait()
 
 
 def shards(templates, strain, inverse_psd, antenna, delays):
@@ -480,19 +501,19 @@
             pltpu.VMEM((2, ZS, 2, 16, 128), BF16),
             pltpu.VMEM((2, 256, 128), F32),
             pltpu.VMEM((SKY, 8, 128), F32),
-            pltpu.VMEM((ZS, 16, 128), F32),
-            pltpu.VMEM((ZS, 16, 128), F32),
+            pltpu.VMEM((ZS, 8, 128), F32),
+            pltpu.VMEM((ZS, 8, 128), F32),
             pltpu.VMEM((8, 128), F32),
-            pltpu.VMEM((CELLS, 8, 128), F32),
+            pltpu.VMEM((CELLS * ZS, 128), F32),
             dma((6,)), dma((NCHUNK,)),
             dma((GROUPS - 1,)), dma((GROUPS - 1,)),
             pltpu.VMEM((48, CHUNK), BF16),
             dma, dma,
-            regular, regular, regular, regular,
+            regular, regular, regular, regular, regular, regular,
             dma((2, CELLS - 1)), dma((2, CELLS - 1)),
-            dma((2, ZS - 1)), dma((2, ZS - 1)),
-            dma((ZS - 1,)), dma((ZS - 1,)),
-            dma((CELLS - 1,)), dma((CELLS - 1,)),
+            dma((2, ZS - 1)), dma((2, ZS)),
+            dma((ZS - 1,)), dma((ZS,)),
+            dma, dma,
         ],
         compiler_params=pltpu.CompilerParams(
             collective_id=0, has_side_effects=True, vmem_limit_bytes=60 * 1024 * 1024
@@ -507,6 +528,16 @@
         tab,
         last,
     )
+    sky, peak = pl.pallas_call(
+        hand_over,
+        out_shape=(
+            jax.ShapeDtypeStruct((8, LEN), F32),
+            jax.ShapeDtypeStruct((1, SKY), F32),
+        ),
+        in_specs=[hbm, hbm],
+        out_specs=(hbm, hbm),
+        scratch_shapes=[dma((2,))],
+    )(sky, peak)
     return (sky[None], peak)
 
 

time: 54.7 us -> 49.6 us (0.907)
  the two profiles are of different devices: /device:TPU:480 before, /device:TPU:1 now
where the time goes in v3:
time: 49.6 us; the launch traced here: 49.5 us
  Pallas kernels  48.9 us (99%)
  between operations  0.64 us (1%)
    pallas_call x1, Pallas kernels, shards(): pl.pallas_call(kernel, out_shape=(jax.ShapeDtypeStruct((8, LEN), F32), ja...  46.8 us
    pallas_call x1, Pallas kernels, shards(): pl.pallas_call(hand_over, out_shape=(jax.ShapeDtypeStruct((8, LEN), F32),...  2.13 us

profile of v3, /device:TPU:1, one launch (start us, length us, event | category | flops | bytes accessed | tf_op | source)
XLA Modules:
  0.0 49.5 jit_solution(9221452538304454636)
XLA Ops:
  0.6 46.8 %shard_map.86 = (f32[8,1024]{1,0:T(8,128)}, f32[1,64]{1,0:T(1,128)}) custom-call(bf16[16,1024]{1,0:T(8,128)(2,1)} %bitcast.5, bf16[48,256]{1,0:T(8,128)(2,1)} %bitcast.6, f32[24,1024]{1,0:T(8,128)} %bitcast.4, f32[3,64]{1,0:T(4,128)} %ant_hbm.1, s32[3,64]{1,0:T(4,128)} %delay_hbm.1, bf16[5,1024,512]{2,1,0:T(8,128)(2,1)} %constant.4.clone.tab_hbm, ...), custom_call_target="tpu_custom_call" | custom-call | flops 400000000 | bytes 6000000 | tf_op jit(solution)/shard_map/pallas_call | solution.py:478
  47.4 2.1 %shard_map.87 = (f32[8,1024]{1,0:T(8,128)}, f32[1,64]{1,0:T(1,128)}) custom-call(f32[8,1024]{1,0:T(8,128)} %get-tuple-element.6.sky_in, f32[1,64]{1,0:T(1,128)} %get-tuple-element.7.peak_in), custom_call_target="tpu_custom_call" | custom-call | tf_op jit(solution)/shard_map/pallas_call | solution.py:531

commit v4 on v3

--- a/solution.py
+++ b/solution.py
@@ -28,6 +28,7 @@
 NCHUNK = COLS // CHUNK
 SIG = 16
 LANES = SIG + DET * WIDE
+UNROLL = 4
 
 
 def section_one_table():
@@ -124,7 +125,7 @@
     sky_out, peak_out,
     ant, delay, tmpl_v, strain_v, psd_v, tab_v, last_v, acc_v, twist_v, turn_v, turn2_v,
     send_xy, recv_xy, send_z, recv_z, fin_v, pk_v, send_r, recv_r, send_p, recv_p,
-    load_sem, tab_sem, s_send, s_recv, relay_v, relay_send, relay_recv, hello, hello_relay, ready_xy, ready_z, go_xy, go_z, xy_send, xy_recv, z_send, z_recv, r_send, r_recv, p_send, p_recv,
+    load_sem, tab_sem, s_send, s_recv, relay_v, relay_send, relay_recv, hello, ready, go, xy_send, xy_recv, z_send, z_recv, r_send, r_recv, p_send, p_recv,
 ):
     t = lax.axis_index("tmpl")
     g = lax.axis_index("det")
@@ -138,7 +139,13 @@
     diag_g = lax.rem(core_g + 2, GROUPS)
     core_id = {"tmpl": t, "det": core_g}
     far_id = {"tmpl": t, "det": far_g}
-    cell_to = [lax.rem(cell + k, CELLS) for k in range(1, CELLS)]
+    side = 4
+    offsets = sorted(
+        ((a, b) for a in range(side) for b in range(side) if a or b),
+        key=lambda o: -min(o[0], side - o[0]) - min(o[1], side - o[1]),
+    )
+    cell_x, cell_y = lax.div(cell, side), lax.rem(cell, side)
+    cell_to = [lax.rem(cell_x + a, side) * side + lax.rem(cell_y + b, side) for a, b in offsets]
     xy_ids = [{"tmpl": c * ZS + z, "det": g} for c in cell_to]
     z_to = z_far_first(z)
     z_ids = [{"tmpl": cell * ZS + k, "det": g} for k in z_to]
@@ -146,6 +153,10 @@
     def signal(sem, who):
         pl.semaphore_signal(sem, inc=1, device_id=who, device_id_type=MESH)
 
+    step = ZS // 2
+    above_id = {"tmpl": t + step, "det": g}
+    far_above_id = {"tmpl": t + step, "det": far_g}
+    near_ids = [{"tmpl": cell * ZS + lax.rem(z + k, step), "det": g} for k in range(1, step)]
     barrier = pltpu.get_barrier_semaphore()
 
     @pl.when(late == 0)
@@ -153,7 +164,7 @@
         @pl.when(near_z)
         def _():
             signal(barrier, far_id)
-            signal(barrier, {"tmpl": t + ZS // 2, "det": far_g})
+            signal(barrier, far_above_id)
 
     signal(barrier, core_id)
 
@@ -161,6 +172,35 @@
     def _():
         for who in z_ids + xy_ids:
             signal(barrier, who)
+
+    def remote(source, target, send, recv, who):
+        return pltpu.make_async_remote_copy(
+            src_ref=source, dst_ref=target, send_sem=send, recv_sem=recv, device_id=who, device_id_type=MESH
+        )
+
+    to_core = remote(strain_hbm, strain_v.at[g], s_send.at[0], s_recv.at[0], core_id)
+    to_far = remote(strain_hbm, strain_v.at[g], s_send.at[1], s_recv.at[1], far_id)
+    down_far = remote(strain_hbm, relay_v.at[0], s_send.at[1], relay_recv.at[0], {"tmpl": t - step, "det": far_g})
+    down = remote(strain_hbm, relay_v.at[1], s_send.at[1], relay_recv.at[1], {"tmpl": t - step, "det": g})
+    up = remote(relay_v.at[0], strain_v.at[far_g], relay_send.at[0], s_recv.at[1], above_id)
+    up_far = remote(relay_v.at[1], strain_v.at[g], relay_send.at[1], s_recv.at[1], far_above_id)
+    handed_on = remote(strain_v.at[far_g], strain_v.at[far_g], s_send.at[2], s_recv.at[2], core_id)
+    is_near = jnp.logical_and(late == 0, near_z)
+
+    @pl.when(late == 1)
+    def _():
+        pl.semaphore_wait(barrier, 2)
+
+        @pl.when(near_z)
+        def _():
+            to_far.start()
+            signal(hello, far_id)
+
+        @pl.when(jnp.logical_not(near_z))
+        def _():
+            down_far.start()
+
+        to_core.start()
 
     loads = [
         pltpu.make_async_copy(strain_hbm, strain_v.at[g], load_sem.at[0]),
@@ -174,42 +214,6 @@
     for copy in loads + tab_loads:
         copy.start()
 
-    def remote(source, target, send, recv, who):
-        return pltpu.make_async_remote_copy(
-            src_ref=source, dst_ref=target, send_sem=send, recv_sem=recv, device_id=who, device_id_type=MESH
-        )
-
-    to_core = remote(strain_hbm, strain_v.at[g], s_send.at[0], s_recv.at[0], core_id)
-    to_far = remote(strain_hbm, strain_v.at[g], s_send.at[1], s_recv.at[1], far_id)
-    to_relay = remote(strain_hbm, relay_v, s_send.at[1], relay_recv, {"tmpl": t - ZS // 2, "det": far_g})
-    relayed = remote(relay_v, strain_v.at[far_g], relay_send, s_recv.at[1], {"tmpl": t + ZS // 2, "det": g})
-    handed_on = remote(strain_v.at[far_g], strain_v.at[far_g], s_send.at[2], s_recv.at[2], core_id)
-
-    @pl.when(late == 0)
-    def _():
-        pl.semaphore_wait(barrier, 1 + (ZS - 1) + (CELLS - 1))
-
-        @pl.when(near_z)
-        def _():
-            pl.semaphore_wait(hello_relay, 1)
-            signal(hello, {"tmpl": t + ZS // 2, "det": g})
-
-    @pl.when(late == 1)
-    def _():
-        pl.semaphore_wait(barrier, 2)
-
-        @pl.when(near_z)
-        def _():
-            signal(hello, far_id)
-            to_far.start()
-
-        @pl.when(jnp.logical_not(near_z))
-        def _():
-            signal(hello_relay, {"tmpl": t - ZS // 2, "det": far_g})
-            to_relay.start()
-
-    to_core.start()
-
     row = lax.broadcasted_iota(jnp.int32, (ROWS, COLS), 0)
     col = lax.broadcasted_iota(jnp.int32, (ROWS, COLS), 1)
     sample = col - 2 * HALO * ((col * 52429) >> 22) - HALO
@@ -241,23 +245,28 @@
             for copy in tab_loads:
                 copy.wait()
         elif order == 1:
+
+            @pl.when(late == 0)
+            def _():
+                pl.semaphore_wait(barrier, 1 + (ZS - 1) + (CELLS - 1))
+
+                @pl.when(near_z)
+                def _():
+                    down_far.wait_recv()
+                    up.start()
+                    to_core.start()
+                    pl.semaphore_wait(hello, 1)
+                    to_far.start()
+                    for who in near_ids + xy_ids:
+                        signal(ready, who)
+
+                @pl.when(jnp.logical_not(near_z))
+                def _():
+                    down.start()
+                    to_core.start()
+
             to_core.wait_recv()
         elif order == 2:
-
-            @pl.when(jnp.logical_and(late == 0, near_z))
-            def _():
-                to_relay.wait_recv()
-                relayed.start()
-
-            @pl.when(late == 0)
-            def _():
-                pl.semaphore_wait(hello, 1)
-                to_far.start()
-                for who in xy_ids:
-                    signal(ready_xy, who)
-                for who in z_ids:
-                    signal(ready_z, who)
-
             to_far.wait_recv()
             handed_on.start()
         else:
@@ -306,35 +315,28 @@
 
     @pl.when(late == 1)
     def _():
-        pl.semaphore_wait(go_xy, 1)
-
-    xy_copies = []
+        pl.semaphore_wait(go, 1)
+
+    xy_copies = [
+        remote(send_xy.at[:, cell_to[k]], recv_xy.at[:, cell], xy_send.at[k], xy_recv.at[k], xy_ids[k])
+        for k in range(CELLS - 1)
+    ]
+    for copy in xy_copies:
+        copy.start()
+    recv_xy[:, cell] = send_xy[:, cell]
+
+    @pl.when(is_near)
+    def _():
+        down.wait_recv()
+        up_far.start()
+        pl.semaphore_wait(ready, (step - 1) + (CELLS - 1))
+        signal(go, far_id)
+        signal(go, far_above_id)
+
+    lane = lax.broadcasted_iota(jnp.int32, (ROWS, 128), 1)
+    for copy in xy_copies:
+        copy.wait_recv()
     for part in range(2):
-        copies = [
-            pltpu.make_async_remote_copy(
-                src_ref=send_xy.at[part, cell_to[k]], dst_ref=recv_xy.at[part, cell],
-                send_sem=xy_send.at[part, k], recv_sem=xy_recv.at[part, k],
-                device_id=xy_ids[k], device_id_type=MESH,
-            )
-            for k in range(CELLS - 1)
-        ]
-        for copy in copies:
-            copy.start()
-        xy_copies.append(copies)
-        recv_xy[part, cell] = send_xy[part, cell]
-
-    @pl.when(late == 0)
-    def _():
-        pl.semaphore_wait(ready_xy, CELLS - 1)
-        signal(go_xy, far_id)
-        pl.semaphore_wait(ready_z, ZS - 1)
-        signal(go_z, far_id)
-
-    lane = lax.broadcasted_iota(jnp.int32, (ROWS, 128), 1)
-    z_copies = []
-    for part in range(2):
-        for copy in xy_copies[part]:
-            copy.wait_recv()
         cells = []
         for c in range(CELLS):
             value = recv_xy[part, c].astype(F32)
@@ -350,29 +352,18 @@
                 yr = jnp.where(lane < SIG, high, yr)
                 yi = jnp.where(lane < SIG, low, yi)
             send_z[part, q] = jnp.concatenate([yr, yi], axis=0).astype(BF16)
-        copies = [
-            pltpu.make_async_remote_copy(
-                src_ref=send_z.at[part, pl.ds(2 * z_to[k], 2)], dst_ref=recv_z.at[part, z],
-                send_sem=z_send.at[part, k], recv_sem=z_recv.at[part, z],
-                device_id=z_ids[k], device_id_type=MESH,
-            )
-            for k in range(ZS - 1)
-        ]
-        if part == 0:
-
-            @pl.when(late == 1)
-            def _():
-                pl.semaphore_wait(go_z, 1)
-
-        for copy in copies:
-            copy.start()
-        z_copies.append(copies)
-        recv_z[part, z] = send_z[part, pl.ds(2 * z, 2)]
+    z_copies = [
+        remote(send_z.at[:, pl.ds(2 * z_to[k], 2)], recv_z.at[:, z], z_send.at[k], z_recv.at[z], z_ids[k])
+        for k in range(ZS - 1)
+    ]
+    for copy in z_copies:
+        copy.start()
+    recv_z[:, z] = send_z[:, pl.ds(2 * z, 2)]
 
     scales = None
+    for k in z_to:
+        pltpu.make_async_copy(recv_z.at[:, k], recv_z.at[:, k], z_recv.at[k]).wait()
     for part in range(2):
-        for k in z_to:
-            pltpu.make_async_copy(recv_z.at[part, k], recv_z.at[part, k], z_recv.at[part, k]).wait()
         got = recv_z[part].reshape(256, 128)
         if part == 0:
             halves = recv_z[part, :, 0].astype(F32)
@@ -402,7 +393,28 @@
 
     loads[4].wait()
     loads[5].wait()
-    best = lax.fori_loop(0, SKY, visit, jnp.zeros((64, 128), F32))
+    def visits(n, best):
+        for k in range(UNROLL):
+            best = visit(UNROLL * n + k, best)
+        return best
+
+    best = lax.fori_loop(0, SKY // UNROLL, visits, jnp.zeros((64, 128), F32))
+
+    tops = jnp.max(pk_v[...], axis=1)
+    tops = jnp.max(jnp.transpose(tops), axis=0, keepdims=True)
+    tops = jnp.concatenate([tops, jnp.zeros((1, 128 - SKY), F32)], axis=1)
+    send_p[...] = jnp.broadcast_to(tops, (8, 128))
+    others = CELLS * ZS - 1
+
+    for place in z_to + [z]:
+
+        def tell(k, carry):
+            who = {"tmpl": lax.rem(cell + k, CELLS) * ZS + place, "det": g}
+            remote(send_p.at[pl.ds(0, 1)], recv_p.at[pl.ds(t, 1)], p_send, p_recv, who).start()
+            return carry
+
+        lax.fori_loop(1 if place is z else 0, CELLS, tell, 0)
+    recv_p[pl.ds(t, 1), :] = tops
 
     for k in range(ZS):
         send_r[k] = best[8 * k : 8 * k + 8]
@@ -412,20 +424,6 @@
     for copy in r_copies:
         copy.start()
     recv_r[z] = send_r[z]
-
-    tops = jnp.max(pk_v[...], axis=1)
-    tops = jnp.max(jnp.transpose(tops), axis=0, keepdims=True)
-    tops = jnp.concatenate([tops, jnp.zeros((1, 128 - SKY), F32)], axis=1)
-    send_p[...] = jnp.broadcast_to(tops, (8, 128))
-    others = CELLS * ZS - 1
-
-    def tell(k, carry):
-        who = lax.rem(t + k, CELLS * ZS)
-        remote(send_p.at[pl.ds(0, 1)], recv_p.at[pl.ds(t, 1)], p_send, p_recv, {"tmpl": who, "det": g}).start()
-        return carry
-
-    lax.fori_loop(1, CELLS * ZS, tell, 0)
-    recv_p[pl.ds(t, 1), :] = tops
 
     for k in z_to:
         pltpu.make_async_copy(recv_r.at[k], recv_r.at[k], r_recv.at[k]).wait()
@@ -446,11 +444,12 @@
     for copy in (to_core, to_far, handed_on):
         copy.wait_send()
 
-    @pl.when(jnp.logical_and(late == 0, near_z))
+    @pl.when(is_near)
     def _():
-        relayed.wait_send()
-
-    for copy in xy_copies[0] + xy_copies[1] + z_copies[0] + z_copies[1] + r_copies:
+        up.wait_send()
+        up_far.wait_send()
+
+    for copy in xy_copies + z_copies + r_copies:
         copy.wait_send()
     pltpu.make_async_copy(recv_p.at[rows], recv_p.at[rows], p_send).wait()
 
@@ -472,15 +471,13 @@
     tab = jnp.asarray(section_one_table())
     last = jnp.asarray(last_section_table())
     hbm = pl.BlockSpec(memory_space=pltpu.HBM)
+    anywhere = pl.BlockSpec(memory_space=pl.ANY)
     vmem = pl.BlockSpec(memory_space=pltpu.VMEM)
     dma = pltpu.SemaphoreType.DMA
     regular = pltpu.SemaphoreType.REGULAR
     sky, peak = pl.pallas_call(
         kernel,
-        out_shape=(
-            jax.ShapeDtypeStruct((8, LEN), F32),
-            jax.ShapeDtypeStruct((1, SKY), F32),
-        ),
+        out_shape=(pltpu.VMEM((8, LEN), F32), pltpu.VMEM((1, SKY), F32)),
         in_specs=[hbm] * 7,
         out_specs=(vmem, vmem),
         scratch_shapes=[
@@ -507,16 +504,16 @@
             pltpu.VMEM((CELLS * ZS, 128), F32),
             dma((6,)), dma((NCHUNK,)),
             dma((GROUPS - 1,)), dma((GROUPS - 1,)),
-            pltpu.VMEM((48, CHUNK), BF16),
-            dma, dma,
-            regular, regular, regular, regular, regular, regular,
-            dma((2, CELLS - 1)), dma((2, CELLS - 1)),
-            dma((2, ZS - 1)), dma((2, ZS)),
+            pltpu.VMEM((2, 48, CHUNK), BF16),
+            dma((2,)), dma((2,)),
+            regular, regular, regular,
+            dma((CELLS - 1,)), dma((CELLS - 1,)),
+            dma((ZS - 1,)), dma((ZS,)),
             dma((ZS - 1,)), dma((ZS,)),
             dma, dma,
         ],
         compiler_params=pltpu.CompilerParams(
-            collective_id=0, has_side_effects=True, vmem_limit_bytes=60 * 1024 * 1024
+            collective_id=0, has_side_effects=True, vmem_limit_bytes=56 * 1024 * 1024
         ),
         cost_estimate=pl.CostEstimate(flops=400_000_000, bytes_accessed=6_000_000, transcendentals=0),
     )(
@@ -530,13 +527,11 @@
     )
     sky, peak = pl.pallas_call(
         hand_over,
-        out_shape=(
-            jax.ShapeDtypeStruct((8, LEN), F32),
-            jax.ShapeDtypeStruct((1, SKY), F32),
-        ),
-        in_specs=[hbm, hbm],
-        out_specs=(hbm, hbm),
+        out_shape=(jax.ShapeDtypeStruct((8, LEN), F32), jax.ShapeDtypeStruct((1, SKY), F32)),
+        in_specs=[anywhere, anywhere],
+        out_specs=(anywhere, anywhere),
         scratch_shapes=[dma((2,))],
+        compiler_params=pltpu.CompilerParams(vmem_limit_bytes=1024 * 1024),
     )(sky, peak)
     return (sky[None], peak)
 

time: 49.6 us -> 46 us (0.927)
  Pallas kernels: 48.9 us -> 45.3 us
    pallas_call x1, Pallas kernels: 46.8 us -> 44.6 us  [shards(): pl.pallas_call(kernel, out_shape=(pltpu.VMEM((8, LEN), F32), pltpu.VMEM((...]
    pallas_call x1, Pallas kernels: 2.13 us -> 0.64 us  [shards(): pl.pallas_call(hand_over, out_shape=(jax.ShapeDtypeStruct((8, LEN), F32),...]
where the time goes in v4:
time: 46 us; the launch traced here: 45.9 us
  Pallas kernels  45.3 us (98%)
  between operations  0.64 us (1%)
    pallas_call x1, Pallas kernels, shards(): pl.pallas_call(kernel, out_shape=(pltpu.VMEM((8, LEN), F32), pltpu.VMEM((...  44.6 us

profile of v4, /device:TPU:1, one launch (start us, length us, event | category | flops | bytes accessed | tf_op | source)
XLA Modules:
  0.0 45.9 jit_solution(3396962163139101722)
XLA Ops:
  0.6 44.6 %shard_map.86 = (f32[8,1024]{1,0:T(8,128)S(1)}, f32[1,64]{1,0:T(1,128)S(1)}) custom-call(bf16[16,1024]{1,0:T(8,128)(2,1)} %bitcast.5, bf16[48,256]{1,0:T(8,128)(2,1)} %bitcast.6, f32[24,1024]{1,0:T(8,128)} %bitcast.4, f32[3,64]{1,0:T(4,128)} %ant_hbm.1, s32[3,64]{1,0:T(4,128)} %delay_hbm.1, bf16[5,1024,512]{2,1,0:T(8,128)(2,1)} %constant.4.clone.tab_hbm, ...), custom_call_target="tpu_custom_call" | custom-call | flops 400000000 | bytes 6000000 | tf_op jit(solution)/shard_map/pallas_call | solution.py:478
  45.3 0.6 %shard_map.87 = (f32[8,1024]{1,0:T(8,128)}, f32[1,64]{1,0:T(1,128)}) custom-call(f32[8,1024]{1,0:T(8,128)S(1)} %get-tuple-element.6.sky_in, f32[1,64]{1,0:T(1,128)S(1)} %get-tuple-element.7.peak_in), custom_call_target="tpu_custom_call" | custom-call | tf_op jit(solution)/shard_map/pallas_call | solution.py:528

commit v5 on v4

--- a/solution.py
+++ b/solution.py
@@ -154,6 +154,9 @@
         pl.semaphore_signal(sem, inc=1, device_id=who, device_id_type=MESH)
 
     step = ZS // 2
+    middle = jnp.logical_and(z >= step, z < step + 2)
+    top = z >= step + 2
+    below_top = jnp.logical_and(z >= 2, z < step)
     above_id = {"tmpl": t + step, "det": g}
     far_above_id = {"tmpl": t + step, "det": far_g}
     near_ids = [{"tmpl": cell * ZS + lax.rem(z + k, step), "det": g} for k in range(1, step)]
@@ -165,6 +168,14 @@
         def _():
             signal(barrier, far_id)
             signal(barrier, far_above_id)
+
+        @pl.when(middle)
+        def _():
+            signal(barrier, far_id)
+
+        @pl.when(top)
+        def _():
+            signal(barrier, {"tmpl": t - step, "det": core_g})
 
     signal(barrier, core_id)
 
@@ -184,19 +195,28 @@
     down = remote(strain_hbm, relay_v.at[1], s_send.at[1], relay_recv.at[1], {"tmpl": t - step, "det": g})
     up = remote(relay_v.at[0], strain_v.at[far_g], relay_send.at[0], s_recv.at[1], above_id)
     up_far = remote(relay_v.at[1], strain_v.at[g], relay_send.at[1], s_recv.at[1], far_above_id)
+    up_other = remote(
+        relay_v.at[0], strain_v.at[far_g], relay_send.at[2], s_recv.at[2], {"tmpl": t + step, "det": core_g}
+    )
     handed_on = remote(strain_v.at[far_g], strain_v.at[far_g], s_send.at[2], s_recv.at[2], core_id)
     is_near = jnp.logical_and(late == 0, near_z)
+    hands_on = jnp.logical_or(late == 1, z < step + 2)
 
     @pl.when(late == 1)
     def _():
-        pl.semaphore_wait(barrier, 2)
+        pl.semaphore_wait(barrier, jnp.where(middle, 3, 2))
 
         @pl.when(near_z)
         def _():
             to_far.start()
             signal(hello, far_id)
 
-        @pl.when(jnp.logical_not(near_z))
+        @pl.when(middle)
+        def _():
+            to_far.start()
+            signal(hello, {"tmpl": t - step, "det": far_g})
+
+        @pl.when(top)
         def _():
             down_far.start()
 
@@ -248,14 +268,18 @@
 
             @pl.when(late == 0)
             def _():
-                pl.semaphore_wait(barrier, 1 + (ZS - 1) + (CELLS - 1))
+                pl.semaphore_wait(barrier, 1 + (ZS - 1) + (CELLS - 1) + jnp.where(below_top, 1, 0))
 
                 @pl.when(near_z)
                 def _():
-                    down_far.wait_recv()
-                    up.start()
+                    @pl.when(below_top)
+                    def _():
+                        down_far.wait_recv()
+                        up.start()
+                        up_other.start()
+
                     to_core.start()
-                    pl.semaphore_wait(hello, 1)
+                    pl.semaphore_wait(hello, jnp.where(below_top, 1, 2))
                     to_far.start()
                     for who in near_ids + xy_ids:
                         signal(ready, who)
@@ -268,7 +292,11 @@
             to_core.wait_recv()
         elif order == 2:
             to_far.wait_recv()
-            handed_on.start()
+
+            @pl.when(hands_on)
+            def _():
+                handed_on.start()
+
         else:
             handed_on.wait_recv()
         lanes = pl.ds(pl.multiple_of(CHUNK * piece, CHUNK), CHUNK)
@@ -406,14 +434,17 @@
     send_p[...] = jnp.broadcast_to(tops, (8, 128))
     others = CELLS * ZS - 1
 
-    for place in z_to + [z]:
-
-        def tell(k, carry):
-            who = {"tmpl": lax.rem(cell + k, CELLS) * ZS + place, "det": g}
-            remote(send_p.at[pl.ds(0, 1)], recv_p.at[pl.ds(t, 1)], p_send, p_recv, who).start()
-            return carry
-
-        lax.fori_loop(1 if place is z else 0, CELLS, tell, 0)
+    own = jnp.where(late == 0, z, ZS - 1 - z) * CELLS + cell
+
+    def tell(k, carry):
+        turn = k + jnp.where(k >= own, 1, 0)
+        place = lax.div(turn, CELLS)
+        place = jnp.where(late == 0, place, ZS - 1 - place)
+        who = {"tmpl": lax.rem(turn, CELLS) * ZS + place, "det": g}
+        remote(send_p.at[pl.ds(0, 1)], recv_p.at[pl.ds(t, 1)], p_send, p_recv, who).start()
+        return carry
+
+    lax.fori_loop(0, others, tell, 0)
     recv_p[pl.ds(t, 1), :] = tops
 
     for k in range(ZS):
@@ -441,13 +472,21 @@
     pltpu.make_async_copy(recv_p.at[rows], recv_p.at[rows], p_recv).wait()
     peak_out[...] = jnp.max(recv_p[...], axis=0, keepdims=True)[:, :SKY]
 
-    for copy in (to_core, to_far, handed_on):
+    for copy in (to_core, to_far):
         copy.wait_send()
 
+    @pl.when(hands_on)
+    def _():
+        handed_on.wait_send()
+
     @pl.when(is_near)
     def _():
-        up.wait_send()
         up_far.wait_send()
+
+        @pl.when(below_top)
+        def _():
+            up.wait_send()
+            up_other.wait_send()
 
     for copy in xy_copies + z_copies + r_copies:
         copy.wait_send()
@@ -505,7 +544,7 @@
             dma((6,)), dma((NCHUNK,)),
             dma((GROUPS - 1,)), dma((GROUPS - 1,)),
             pltpu.VMEM((2, 48, CHUNK), BF16),
-            dma((2,)), dma((2,)),
+            dma((3,)), dma((2,)),
             regular, regular, regular,
             dma((CELLS - 1,)), dma((CELLS - 1,)),
             dma((ZS - 1,)), dma((ZS,)),

time: 46 us -> 45.6 us (level)
  Pallas kernels: 45.3 us -> 44.8 us
    pallas_call x1, Pallas kernels: 44.6 us -> 44.2 us  [shards(): pl.pallas_call(kernel, out_shape=(pltpu.VMEM((8, LEN), F32), pltpu.VMEM((...]
where the time goes in v5:
time: 45.6 us; the launch traced here: 45.4 us
  Pallas kernels  44.8 us (98%)
  between operations  0.64 us (1%)
    pallas_call x1, Pallas kernels, shards(): pl.pallas_call(kernel, out_shape=(pltpu.VMEM((8, LEN), F32), pltpu.VMEM((...  44.2 us

profile of v5, /device:TPU:1, one launch (start us, length us, event | category | flops | bytes accessed | tf_op | source)
XLA Modules:
  0.0 45.4 jit_solution(9958394190673204870)
XLA Ops:
  0.6 44.2 %shard_map.86 = (f32[8,1024]{1,0:T(8,128)S(1)}, f32[1,64]{1,0:T(1,128)S(1)}) custom-call(bf16[16,1024]{1,0:T(8,128)(2,1)} %bitcast.5, bf16[48,256]{1,0:T(8,128)(2,1)} %bitcast.6, f32[24,1024]{1,0:T(8,128)} %bitcast.4, f32[3,64]{1,0:T(4,128)} %ant_hbm.1, s32[3,64]{1,0:T(4,128)} %delay_hbm.1, bf16[5,1024,512]{2,1,0:T(8,128)(2,1)} %constant.4.clone.tab_hbm, ...), custom_call_target="tpu_custom_call" | custom-call | flops 400000000 | bytes 6000000 | tf_op jit(solution)/shard_map/pallas_call | solution.py:517
  44.8 0.6 %shard_map.87 = (f32[8,1024]{1,0:T(8,128)}, f32[1,64]{1,0:T(1,128)}) custom-call(f32[8,1024]{1,0:T(8,128)S(1)} %get-tuple-element.6.sky_in, f32[1,64]{1,0:T(1,128)S(1)} %get-tuple-element.7.peak_in), custom_call_target="tpu_custom_call" | custom-call | tf_op jit(solution)/shard_map/pallas_call | solution.py:567

commit v6 on v5

--- a/solution.py
+++ b/solution.py
@@ -28,7 +28,7 @@
 NCHUNK = COLS // CHUNK
 SIG = 16
 LANES = SIG + DET * WIDE
-UNROLL = 4
+SCAN = 16
 
 
 def section_one_table():
@@ -124,7 +124,7 @@
     tmpl_hbm, strain_hbm, psd_hbm, ant_hbm, delay_hbm, tab_hbm, last_hbm,
     sky_out, peak_out,
     ant, delay, tmpl_v, strain_v, psd_v, tab_v, last_v, acc_v, twist_v, turn_v, turn2_v,
-    send_xy, recv_xy, send_z, recv_z, fin_v, pk_v, send_r, recv_r, send_p, recv_p,
+    send_xy, recv_xy, send_z, recv_z, sky_v, fin_v, pk_v, send_r, recv_r, send_p, recv_p,
     load_sem, tab_sem, s_send, s_recv, relay_v, relay_send, relay_recv, hello, ready, go, xy_send, xy_recv, z_send, z_recv, r_send, r_recv, p_send, p_recv,
 ):
     t = lax.axis_index("tmpl")
@@ -257,6 +257,19 @@
     ]
     blank = jnp.zeros((ROWS, SIG - DET), F32)
     sig = [jnp.concatenate([parts[d][c] for d in range(DET)] + [blank], axis=1) for c in range(2)]
+
+    loads[4].wait()
+    loads[5].wait()
+    distance = lax.broadcasted_iota(jnp.int32, (64, 256), 1) - lax.broadcasted_iota(jnp.int32, (64, 256), 0)
+
+    def weigh(s, carry):
+        weights = jnp.zeros((64, 256), F32)
+        for d in range(DET):
+            weights = jnp.where(distance == SIG + WIDE * d + HALO + delay[d, s], ant[d, s], weights)
+        sky_v[pl.ds(pl.multiple_of(64 * s, 64), 64), :] = weights.astype(BF16)
+        return carry
+
+    lax.fori_loop(0, SKY, weigh, 0)
 
     half = DET * ROWS
     for order, piece in enumerate([g, core_g, far_g, diag_g]):
@@ -403,30 +416,17 @@
             high_row = min(SIG + WIDE * (d + 1), 128 * part + 128)
             if low_row < high_row:
                 block = out[low_row - 128 * part : high_row - 128 * part]
-                fin_v[0, low_row:high_row, :] = block[:, :128] * scales[d]
-                fin_v[1, low_row:high_row, :] = block[:, 128:] * scales[d]
-
-    def visit(s, best):
-        sum_r = sum_i = None
-        for d in range(DET):
-            rows = pl.ds(SIG + WIDE * d + HALO + delay[d, s], 64)
-            gain = ant[d, s]
-            real = gain * fin_v[0, rows, :]
-            imag = gain * fin_v[1, rows, :]
-            sum_r = real if sum_r is None else sum_r + real
-            sum_i = imag if sum_i is None else sum_i + imag
-        power = sum_r * sum_r + sum_i * sum_i
-        pk_v[s] = jnp.max(power.reshape(8, 8, 128), axis=0)
-        return jnp.maximum(best, power)
-
-    loads[4].wait()
-    loads[5].wait()
-    def visits(n, best):
-        for k in range(UNROLL):
-            best = visit(UNROLL * n + k, best)
-        return best
-
-    best = lax.fori_loop(0, SKY // UNROLL, visits, jnp.zeros((64, 128), F32))
+                fin_v[low_row:high_row, :] = (block * scales[d]).astype(BF16)
+
+    fin_v[:SIG, :] = jnp.zeros((SIG, 256), BF16)
+    detectors = fin_v[...]
+    best = jnp.zeros((64, 128), F32)
+    for first in range(0, SKY, SCAN):
+        both = jnp.dot(sky_v[64 * first : 64 * (first + SCAN), :], detectors, preferred_element_type=F32)
+        real, imag = both[:, :128], both[:, 128:]
+        power = (real * real + imag * imag).reshape(SCAN, 64, 128)
+        pk_v[first : first + SCAN] = jnp.max(power.reshape(SCAN, 8, 8, 128), axis=1)
+        best = jnp.maximum(best, jnp.max(power, axis=0))
 
     tops = jnp.max(pk_v[...], axis=1)
     tops = jnp.max(jnp.transpose(tops), axis=0, keepdims=True)
@@ -535,7 +535,8 @@
             pltpu.VMEM((2, CELLS, 16, 128), BF16),
             pltpu.VMEM((2, 16, 16, 128), BF16),
             pltpu.VMEM((2, ZS, 2, 16, 128), BF16),
-            pltpu.VMEM((2, 256, 128), F32),
+            pltpu.VMEM((SKY * 64, 256), BF16),
+            pltpu.VMEM((256, 256), BF16),
             pltpu.VMEM((SKY, 8, 128), F32),
             pltpu.VMEM((ZS, 8, 128), F32),
             pltpu.VMEM((ZS, 8, 128), F32),

time: 45.6 us -> 44.5 us (0.976)
  Pallas kernels: 44.8 us -> 43.7 us
    pallas_call x1, Pallas kernels: 44.2 us -> 43.1 us  [shards(): pl.pallas_call(kernel, out_shape=(pltpu.VMEM((8, LEN), F32), pltpu.VMEM((...]
where the time goes in v6:
time: 44.5 us; the launch traced here: 44.4 us
  Pallas kernels  43.7 us (98%)
  between operations  0.64 us (1%)
    pallas_call x1, Pallas kernels, shards(): pl.pallas_call(kernel, out_shape=(pltpu.VMEM((8, LEN), F32), pltpu.VMEM((...  43.1 us

profile of v6, /device:TPU:1, one launch (start us, length us, event | category | flops | bytes accessed | tf_op | source)
XLA Modules:
  0.0 44.4 jit_solution(8342520979961209982)
XLA Ops:
  0.6 43.1 %shard_map.86 = (f32[8,1024]{1,0:T(8,128)S(1)}, f32[1,64]{1,0:T(1,128)S(1)}) custom-call(bf16[16,1024]{1,0:T(8,128)(2,1)} %bitcast.5, bf16[48,256]{1,0:T(8,128)(2,1)} %bitcast.6, f32[24,1024]{1,0:T(8,128)} %bitcast.4, f32[3,64]{1,0:T(4,128)} %ant_hbm.1, s32[3,64]{1,0:T(4,128)} %delay_hbm.1, bf16[5,1024,512]{2,1,0:T(8,128)(2,1)} %constant.4.clone.tab_hbm, ...), custom_call_target="tpu_custom_call" | custom-call | flops 400000000 | bytes 6000000 | tf_op jit(solution)/shard_map/pallas_call | solution.py:517
  43.7 0.6 %shard_map.87 = (f32[8,1024]{1,0:T(8,128)}, f32[1,64]{1,0:T(1,128)}) custom-call(f32[8,1024]{1,0:T(8,128)S(1)} %get-tuple-element.6.sky_in, f32[1,64]{1,0:T(1,128)S(1)} %get-tuple-element.7.peak_in), custom_call_target="tpu_custom_call" | custom-call | tf_op jit(solution)/shard_map/pallas_call | solution.py:568

commit v7 on v6

--- a/solution.py
+++ b/solution.py
@@ -266,7 +266,10 @@
         weights = jnp.zeros((64, 256), F32)
         for d in range(DET):
             weights = jnp.where(distance == SIG + WIDE * d + HALO + delay[d, s], ant[d, s], weights)
-        sky_v[pl.ds(pl.multiple_of(64 * s, 64), 64), :] = weights.astype(BF16)
+        high, low = split_two(weights)
+        rows = pl.ds(pl.multiple_of(64 * s, 64), 64)
+        sky_v[rows, :256] = high.astype(BF16)
+        sky_v[rows, 256:] = low.astype(BF16)
         return carry
 
     lax.fori_loop(0, SKY, weigh, 0)
@@ -422,7 +425,9 @@
     detectors = fin_v[...]
     best = jnp.zeros((64, 128), F32)
     for first in range(0, SKY, SCAN):
-        both = jnp.dot(sky_v[64 * first : 64 * (first + SCAN), :], detectors, preferred_element_type=F32)
+        rows = slice(64 * first, 64 * (first + SCAN))
+        both = jnp.dot(sky_v[rows, :256], detectors, preferred_element_type=F32)
+        both = both + jnp.dot(sky_v[rows, 256:], detectors, preferred_element_type=F32)
         real, imag = both[:, :128], both[:, 128:]
         power = (real * real + imag * imag).reshape(SCAN, 64, 128)
         pk_v[first : first + SCAN] = jnp.max(power.reshape(SCAN, 8, 8, 128), axis=1)
@@ -535,7 +540,7 @@
             pltpu.VMEM((2, CELLS, 16, 128), BF16),
             pltpu.VMEM((2, 16, 16, 128), BF16),
             pltpu.VMEM((2, ZS, 2, 16, 128), BF16),
-            pltpu.VMEM((SKY * 64, 256), BF16),
+            pltpu.VMEM((SKY * 64, 512), BF16),
             pltpu.VMEM((256, 256), BF16),
             pltpu.VMEM((SKY, 8, 128), F32),
             pltpu.VMEM((ZS, 8, 128), F32),

time: 44.5 us -> 45 us (1.011)
  Pallas kernels: 43.7 us -> 44.3 us
    pallas_call x1, Pallas kernels: 43.1 us -> 43.6 us  [shards(): pl.pallas_call(kernel, out_shape=(pltpu.VMEM((8, LEN), F32), pltpu.VMEM((...]
where the time goes in v7:
time: 45 us; the launch traced here: 44.9 us
  Pallas kernels  44.3 us (98%)
  between operations  0.64 us (1%)
    pallas_call x1, Pallas kernels, shards(): pl.pallas_call(kernel, out_shape=(pltpu.VMEM((8, LEN), F32), pltpu.VMEM((...  43.6 us

profile of v7, /device:TPU:1, one launch (start us, length us, event | category | flops | bytes accessed | tf_op | source)
XLA Modules:
  0.0 44.9 jit_solution(18017120959810812750)
XLA Ops:
  0.6 43.6 %shard_map.86 = (f32[8,1024]{1,0:T(8,128)S(1)}, f32[1,64]{1,0:T(1,128)S(1)}) custom-call(bf16[16,1024]{1,0:T(8,128)(2,1)} %bitcast.5, bf16[48,256]{1,0:T(8,128)(2,1)} %bitcast.6, f32[24,1024]{1,0:T(8,128)} %bitcast.4, f32[3,64]{1,0:T(4,128)} %ant_hbm.1, s32[3,64]{1,0:T(4,128)} %delay_hbm.1, bf16[5,1024,512]{2,1,0:T(8,128)(2,1)} %constant.4.clone.tab_hbm, ...), custom_call_target="tpu_custom_call" | custom-call | flops 400000000 | bytes 6000000 | tf_op jit(solution)/shard_map/pallas_call | solution.py:522
  44.3 0.6 %shard_map.87 = (f32[8,1024]{1,0:T(8,128)}, f32[1,64]{1,0:T(1,128)}) custom-call(f32[8,1024]{1,0:T(8,128)S(1)} %get-tuple-element.6.sky_in, f32[1,64]{1,0:T(1,128)S(1)} %get-tuple-element.7.peak_in), custom_call_target="tpu_custom_call" | custom-call | tf_op jit(solution)/shard_map/pallas_call | solution.py:573

commit v8 on v6

--- a/solution.py
+++ b/solution.py
@@ -53,7 +53,9 @@
         table[:, ql, 1, :, 0, :, :, ql] = -np.sin(angle)
         table[:, ql, 0, :, 1, :, :, ql] = np.sin(angle)
         table[:, ql, 1, :, 1, :, :, ql] = np.cos(angle)
-    return table.reshape(256, 256).astype(ml_dtypes.bfloat16)
+    table = table.reshape(256, 256)
+    high = table.astype(ml_dtypes.bfloat16)
+    return np.stack([high, (table - high.astype(np.float64)).astype(ml_dtypes.bfloat16)])
 
 
 def unit_circle(turns):
@@ -410,7 +412,11 @@
             halves = recv_z[part, :, 0].astype(F32)
             total = jnp.sum(jnp.sum(halves, axis=0), axis=0, keepdims=True)
             scales = [1.0 / jnp.sqrt(total[:, d : d + 1]) for d in range(DET)]
-        out = lax.dot_general(got, last_v[...] if part else _wait_load(loads[3], last_v), (((0,), (0,)), ((), ())), preferred_element_type=F32)
+        if part == 0:
+            loads[3].wait()
+        out = sum(
+            lax.dot_general(got, last_v[k], (((0,), (0,)), ((), ())), preferred_element_type=F32) for k in range(2)
+        )
         for d in range(DET):
             low_row = max(SIG + WIDE * d, 128 * part)
             high_row = min(SIG + WIDE * (d + 1), 128 * part + 128)
@@ -491,11 +497,6 @@
     for copy in xy_copies + z_copies + r_copies:
         copy.wait_send()
     pltpu.make_async_copy(recv_p.at[rows], recv_p.at[rows], p_send).wait()
-
-
-def _wait_load(copy, ref):
-    copy.wait()
-    return ref[...]
 
 
 def hand_over(sky_in, peak_in, sky_out, peak_out, sem):
@@ -526,7 +527,7 @@
             pltpu.VMEM((GROUPS, 48, CHUNK), BF16),
             pltpu.VMEM((24, LEN), F32),
             pltpu.VMEM((NCHUNK, LEN, 2 * CHUNK), BF16),
-            pltpu.VMEM((256, 256), BF16),
+            pltpu.VMEM((2, 256, 256), BF16),
             pltpu.VMEM((NCHUNK, 48, 2 * CHUNK), F32),
             pltpu.VMEM((2, 24, COLS), F32),
             pltpu.VMEM((2, ROWS, COLS), F32),

time: 44.5 us -> 44.5 us (level)
  no operation moved by 1% of the time
where the time goes in v8:
time: 44.5 us; the launch traced here: 44.4 us
  Pallas kernels  43.8 us (98%)
  between operations  0.64 us (1%)
    pallas_call x1, Pallas kernels, shards(): pl.pallas_call(kernel, out_shape=(pltpu.VMEM((8, LEN), F32), pltpu.VMEM((...  43.2 us

profile of v8, /device:TPU:1, one launch (start us, length us, event | category | flops | bytes accessed | tf_op | source)
XLA Modules:
  0.0 44.4 jit_solution(10785094069936242769)
XLA Ops:
  0.6 43.2 %shard_map.86 = (f32[8,1024]{1,0:T(8,128)S(1)}, f32[1,64]{1,0:T(1,128)S(1)}) custom-call(bf16[16,1024]{1,0:T(8,128)(2,1)} %bitcast.5, bf16[48,256]{1,0:T(8,128)(2,1)} %bitcast.6, f32[24,1024]{1,0:T(8,128)} %bitcast.4, f32[3,64]{1,0:T(4,128)} %ant_hbm.1, s32[3,64]{1,0:T(4,128)} %delay_hbm.1, bf16[5,1024,512]{2,1,0:T(8,128)(2,1)} %constant.4.clone.tab_hbm, ...), custom_call_target="tpu_custom_call" | custom-call | flops 400000000 | bytes 6000000 | tf_op jit(solution)/shard_map/pallas_call | solution.py:518
  43.8 0.6 %shard_map.87 = (f32[8,1024]{1,0:T(8,128)}, f32[1,64]{1,0:T(1,128)}) custom-call(f32[8,1024]{1,0:T(8,128)S(1)} %get-tuple-element.6.sky_in, f32[1,64]{1,0:T(1,128)S(1)} %get-tuple-element.7.peak_in), custom_call_target="tpu_custom_call" | custom-call | tf_op jit(solution)/shard_map/pallas_call | solution.py:569

commit v9 on v7

--- a/solution.py
+++ b/solution.py
@@ -28,7 +28,7 @@
 NCHUNK = COLS // CHUNK
 SIG = 16
 LANES = SIG + DET * WIDE
-SCAN = 16
+SCAN = 64
 
 
 def section_one_table():
@@ -422,12 +422,11 @@
                 fin_v[low_row:high_row, :] = (block * scales[d]).astype(BF16)
 
     fin_v[:SIG, :] = jnp.zeros((SIG, 256), BF16)
-    detectors = fin_v[...]
+    detectors = jnp.concatenate([fin_v[...], fin_v[...]], axis=0)
     best = jnp.zeros((64, 128), F32)
     for first in range(0, SKY, SCAN):
         rows = slice(64 * first, 64 * (first + SCAN))
-        both = jnp.dot(sky_v[rows, :256], detectors, preferred_element_type=F32)
-        both = both + jnp.dot(sky_v[rows, 256:], detectors, preferred_element_type=F32)
+        both = jnp.dot(sky_v[rows, :], detectors, preferred_element_type=F32)
         real, imag = both[:, :128], both[:, 128:]
         power = (real * real + imag * imag).reshape(SCAN, 64, 128)
         pk_v[first : first + SCAN] = jnp.max(power.reshape(SCAN, 8, 8, 128), axis=1)

time: 45 us -> 45 us (level)
  no operation moved by 1% of the time
where the time goes in v9:
time: 45 us; the launch traced here: 44.9 us
  Pallas kernels  44.2 us (98%)
  between operations  0.64 us (1%)
    pallas_call x1, Pallas kernels, shards(): pl.pallas_call(kernel, out_shape=(pltpu.VMEM((8, LEN), F32), pltpu.VMEM((...  43.6 us

profile of v9, /device:TPU:1, one launch (start us, length us, event | category | flops | bytes accessed | tf_op | source)
XLA Modules:
  0.0 44.9 jit_solution(1885084891861192745)
XLA Ops:
  0.6 43.6 %shard_map.86 = (f32[8,1024]{1,0:T(8,128)S(1)}, f32[1,64]{1,0:T(1,128)S(1)}) custom-call(bf16[16,1024]{1,0:T(8,128)(2,1)} %bitcast.5, bf16[48,256]{1,0:T(8,128)(2,1)} %bitcast.6, f32[24,1024]{1,0:T(8,128)} %bitcast.4, f32[3,64]{1,0:T(4,128)} %ant_hbm.1, s32[3,64]{1,0:T(4,128)} %delay_hbm.1, bf16[5,1024,512]{2,1,0:T(8,128)(2,1)} %constant.4.clone.tab_hbm, ...), custom_call_target="tpu_custom_call" | custom-call | flops 400000000 | bytes 6000000 | tf_op jit(solution)/shard_map/pallas_call | solution.py:521
  44.2 0.6 %shard_map.87 = (f32[8,1024]{1,0:T(8,128)}, f32[1,64]{1,0:T(1,128)}) custom-call(f32[8,1024]{1,0:T(8,128)S(1)} %get-tuple-element.6.sky_in, f32[1,64]{1,0:T(1,128)S(1)} %get-tuple-element.7.peak_in), custom_call_target="tpu_custom_call" | custom-call | tf_op jit(solution)/shard_map/pallas_call | solution.py:572
